TPU v7x, 128 devices: a whole 4x4x4 slice. The times are simulated.
128 devices in a mesh: chan: 32 (over x, y_hi, z), win: 4 (over y_lo, core).
Axes of the slice: x: 4, y: 4 (y_hi: 2, y_lo: 2; y = y_hi * 2 + y_lo), z: 4, core: 2. Of those that a mesh axis runs over, the one named last changes fastest.
Arguments:
- records: bfloat16 [256, 1000, 1024], P(('chan', 'win')), may hold values from -50 to 50
Outputs:
- correlations: float32 [1024, 256, 256], P('chan', 'win')
All inputs are finite; a program needn't handle non-finite values.
Results may differ from a plain program's by a relative error of at most 0.0023.
Values may be sent and summed in bfloat16 or wider, within the bound.
No kernel may reach another device: no remote copies, remote signals or barrier semaphores. Data moves between devices by JAX's collectives and lax.ppermute only.
A program may use at most 256 MiB of HBM per device.

v0:
```python
import math

import jax
import jax.numpy as jnp
from jax import lax
from jax.sharding import PartitionSpec as P

SAMPLES = 1000
BINS = 200
FIRST_BIN = 20
BAND = 256
LAGS = 256


def from_behind(block, axis, distance):
    devices = range(lax.axis_size(axis))
    route = [(i - distance, i) for i in devices if i - distance in devices]
    return lax.ppermute(block, axis, route)


def dft_matrix(samples, bin_count):
    times = jnp.arange(samples, dtype=jnp.int32)
    freqs = FIRST_BIN + jnp.arange(bin_count, dtype=jnp.int32)
    turns = times[:, None] * freqs[None, :] % samples
    phase = turns.astype(jnp.float32) * (2.0 * math.pi / samples)
    return jnp.concatenate([jnp.cos(phase), -jnp.sin(phase)], axis=1).astype(jnp.bfloat16)


def lag_matrix(samples, bin_count, lag_count, factor):
    freqs = FIRST_BIN + jnp.arange(bin_count, dtype=jnp.int32)
    shifts = jnp.arange(lag_count, dtype=jnp.int32) - lag_count // 2
    turns = freqs[:, None] * shifts[None, :] % samples
    phase = turns.astype(jnp.float32) * (2.0 * math.pi / samples)
    return jnp.stack([jnp.cos(phase), -jnp.sin(phase)]) * factor


def box_matrix(bin_count):
    places = jnp.arange(bin_count, dtype=jnp.int32)
    near = (jnp.abs(places[:, None] - places[None, :]) <= 4).astype(jnp.float32)
    return near / jnp.sum(near, axis=1, keepdims=True)


def whiten(spectra):
    bin_count = spectra.shape[0] // 2
    real_part = spectra[:bin_count]
    imag_part = spectra[bin_count:]
    power = real_part * real_part + imag_part * imag_part
    smooth = jnp.einsum(
        "jk,kwc->jwc", box_matrix(bin_count), jnp.sqrt(power), precision=lax.Precision.HIGHEST
    )
    level = jnp.sqrt(jnp.mean(power, axis=0, keepdims=True) + 1e-06)
    denom = smooth + 0.25 * level
    return (spectra / jnp.concatenate([denom, denom], axis=0)).astype(jnp.bfloat16)


def skew(part, keep_cols):
    bin_count, row_count, extent = part.shape
    flattened = jnp.pad(part.reshape(bin_count, row_count * extent), ((0, 0), (0, row_count)))
    return flattened.reshape(bin_count, row_count, extent + 1)[:, :, :keep_cols]


def band_stack(left, right, keep_cols):
    bin_count = left.shape[0] // 2
    left_rows = jnp.concatenate([left[:bin_count], left[bin_count:]], axis=1)
    first = jnp.concatenate([right[:bin_count], right[bin_count:]], axis=1)
    second = jnp.concatenate([-right[bin_count:], right[:bin_count]], axis=1)
    right_rows = jnp.concatenate([first, second], axis=2)
    products = jnp.einsum("bwc,bwe->bce", left_rows, right_rows, preferred_element_type=jnp.float32)
    extent = right.shape[2]
    return jnp.stack(
        [skew(products[:, :, :extent], keep_cols), skew(products[:, :, extent:], keep_cols)], axis=1
    )


def per_device(records):
    regrouped = lax.all_to_all(records, "chan", split_axis=2, concat_axis=0, tiled=True)
    window_count = regrouped.shape[0]
    channels = regrouped.shape[2]
    spectra = jnp.einsum(
        "wsc,sf->fwc", regrouped, dft_matrix(SAMPLES, BINS), preferred_element_type=jnp.float32
    )
    whitened = whiten(spectra)
    reach = (BAND + channels - 2) // channels
    pieces = [whitened]
    for hop in range(1, reach + 1):
        pieces.append(from_behind(whitened, "chan", -hop))
    extended = jnp.concatenate(pieces, axis=2)
    groups = lax.axis_size("win")
    lag_table = lag_matrix(SAMPLES, BINS, LAGS, 1.0 / (window_count * groups * math.sqrt(BINS)))
    stacks = band_stack(whitened, extended, BAND)
    partial_sums = jnp.einsum("bpco,pbm->com", stacks, lag_table, precision=lax.Precision.HIGHEST)
    return lax.psum_scatter(partial_sums, "win", scatter_dimension=1, tiled=True)


def solution(mesh):
    in_specs = (P(("chan", "win"), None, None),)
    out_specs = P("chan", "win", None)
    return jax.shard_map(
        per_device, mesh=mesh, in_specs=in_specs, out_specs=out_specs, check_vma=False
    )
```

profile of v0, /device:TPU:21, one launch (start us, length us, event | category | flops | bytes accessed | tf_op | source)
XLA Modules:
  0.0 992.4 jit_solution(17705633578544720873)
XLA Ops:
  6.5 11.4 %copy.11 = bf16[2,1000,1024]{1,0,2:T(2,128)(2,1)} copy(bf16[2,1000,1024]{2,1,0:T(8,128)(2,1)} %param.1) | data formatting | bytes 8192000 | tf_op args[0]
  17.9 10.3 %all-to-all-start = ((bf16[2,1000,1024]{1,0,2:T(2,128)(2,1)}), bf16[2,1000,1024]{1,0,2:T(2,128)(2,1)}, u32[]{:S(2)}, u32[]{:S(2)}) async-start(bf16[2,1000,1024]{1,0,2:T(2,128)(2,1)} %copy.11), calls=%async_computation | async-start | bytes 8388608 | tf_op jit(solution)/shard_map/all_to_all | solution.py:76
  28.4 3.8 cosine_convert_fusion
  32.2 46.1 %all-to-all-done = bf16[2,1000,1024]{1,0,2:T(2,128)(2,1)} async-done(((bf16[2,1000,1024]{1,0,2:T(2,128)(2,1)}), bf16[2,1000,1024]{1,0,2:T(2,128)(2,1)}, u32[]{:S(2)}, u32[]{:S(2)}) %all-to-all-start) | async-done | bytes 4096032 | tf_op jit(solution)/shard_map/all_to_all | solution.py:76
  78.3 3.5 copy.12
  81.8 6.3 copy.13
  88.1 8.3 all_to_all.16
  96.4 4.7 fusion.16
  102.1 2.4 fusion.11
  104.4 2.4 constant_dynamic-update-slice_fusion.8
  106.9 4.5 collective-permute-start
  111.4 6.4 collective-permute-start.1
  117.9 3.4 collective-permute-start.2
  121.3 3.0 collective-permute-start.3
  124.3 2.1 collective-permute-start.4
  126.4 61.2 %collective-permute-done = bf16[400,64,32]{0,1,2:T(8,128)(2,1)S(1)} collective-permute-done((bf16[400,64,32]{0,1,2:T(8,128)(2,1)S(1)}, bf16[400,64,32]{0,1,2:T(8,128)(2,1)S(1)}, u32[]{:S(2)}, u32[]{:S(2)}) %collective-permute-start) | collective-permute-done | bytes 1638432 | tf_op jit(solution)/shard_map/ppermute | solution.py:18
  189.0 1.9 collective-permute-start.5
  190.9 75.4 %collective-permute-done.1 = bf16[400,64,32]{0,1,2:T(8,128)(2,1)S(1)} collective-permute-done((bf16[400,64,32]{0,1,2:T(8,128)(2,1)S(1)}, bf16[400,64,32]{0,1,2:T(8,128)(2,1)S(1)}, u32[]{:S(2)}, u32[]{:S(2)}) %collective-permute-start.1) | collective-permute-done | bytes 1638432 | tf_op jit(solution)/shard_map/ppermute | solution.py:18
  266.3 70.0 %collective-permute-start.6 = (bf16[400,64,32]{0,1,2:T(8,128)(2,1)S(1)}, bf16[400,64,32]{0,1,2:T(8,128)(2,1)}, u32[]{:S(2)}, u32[]{:S(2)}) collective-permute-start(bf16[400,64,32]{0,1,2:T(8,128)(2,1)S(1)} %get-tuple-element.6), channel_id=1, source_target_pairs={{28,0},{32,4},{36,8},{40,12},{44,16},{48,20},{52,24},{56,28},{60,3... | collective-permute-start | bytes 4915208 | tf_op jit(solution)/shard_map/ppermute | solution.py:18
  336.3 1.9 collective-permute-start.7
  339.7 1.8 pad_maximum_fusion
  341.5 4.4 copy.14
  345.8 3.3 constant_dynamic-update-slice_fusion.7
  349.1 3.2 constant_dynamic-update-slice_fusion.6
  353.9 72.0 %collective-permute-done.3 = bf16[400,64,32]{0,1,2:T(8,128)(2,1)} collective-permute-done((bf16[400,64,32]{0,1,2:T(8,128)(2,1)S(1)}, bf16[400,64,32]{0,1,2:T(8,128)(2,1)}, u32[]{:S(2)}, u32[]{:S(2)}) %collective-permute-start.3) | collective-permute-done | bytes 1638432 | tf_op jit(solution)/shard_map/ppermute | solution.py:18
  425.8 3.2 constant_dynamic-update-slice_fusion.4
  429.0 3.1 constant_dynamic-update-slice_fusion.3
  432.2 3.2 constant_dynamic-update-slice_fusion.2
  435.3 7.6 collective-permute-done.6
  442.9 3.1 constant_dynamic-update-slice_fusion.1
  446.0 41.8 %collective-permute-done.7 = bf16[400,64,32]{0,1,2:T(8,128)(2,1)} collective-permute-done((bf16[400,64,32]{0,1,2:T(8,128)(2,1)S(1)}, bf16[400,64,32]{0,1,2:T(8,128)(2,1)}, u32[]{:S(2)}, u32[]{:S(2)}) %collective-permute-start.7) | collective-permute-done | bytes 1638432 | tf_op jit(solution)/shard_map/ppermute | solution.py:18
  487.9 3.1 constant_dynamic-update-slice_fusion
  491.0 18.8 %fusion.44 = (bf16[200,64,288]{0,1,2:T(8,128)(2,1)}, bf16[200,64,288]{0,1,2:T(8,128)(2,1)}, bf16[200,64,288]{0,1,2:T(8,128)(2,1)}) fusion(bf16[400,64,288]{0,1,2:T(8,128)(2,1)} %constant_dynamic-update-slice_fusion), kind=kLoop, calls=%fused_computation.68 | loop fusion | flops 3686400 | bytes 36864000 | tf_op jit(solution)/shard_map/slice | solution.py:65
  509.8 42.1 %maximum_maximum_fusion = bf16[200,128,576]{0,1,2:T(8,128)(2,1)} fusion(bf16[200,64,288]{0,1,2:T(8,128)(2,1)} %get-tuple-element.9, bf16[200,64,288]{0,1,2:T(8,128)(2,1)} %get-tuple-element.8, bf16[200,64,288]{0,1,2:T(8,128)(2,1)} %get-tuple-element.7), kind=kLoop, calls=%fused_computation | loop fusion | flops 117964800 | bytes 51609600 | tf_op jit(solution)/shard_map/concatenate | solution.py:67
  552.0 44.7 %copy.15 = bf16[200,128,576]{1,2,0:T(8,128)(2,1)} copy(bf16[200,128,576]{0,1,2:T(8,128)(2,1)} %maximum_maximum_fusion) | data formatting | bytes 58982400 | tf_op jit(solution)/shard_map/concatenate | solution.py:67
  596.6 20.4 %fusion.47 = f32[200,32,576]{2,1,0:T(8,128)} fusion(bf16[200,128,32]{1,2,0:T(8,128)(2,1)S(1)} %copy-done, bf16[200,128,576]{1,2,0:T(8,128)(2,1)} %copy.15), kind=kOutput, calls=%fused_computation.71 | convolution fusion | flops 943718400 | bytes 45875200 | tf_op jit(solution)/shard_map/bwc,bwe->bce/dot_general | solution.py:68
  617.0 15.6 %fusion.45 = (f32[200,32,288]{2,1,0:T(8,128)}, f32[200,32,288]{2,1,0:T(8,128)}) fusion(f32[200,32,576]{2,1,0:T(8,128)} %fusion.47), kind=kLoop, calls=%fused_computation.69 | loop fusion | bytes 29491200 | tf_op jit(solution)/shard_map/slice | solution.py:71
  632.6 10.0 %reshape.153 = f32[200,9216]{1,0:T(8,128)} reshape(f32[200,32,288]{2,1,0:T(8,128)} %get-tuple-element.11) | data formatting | bytes 14745600 | tf_op jit(solution)/shard_map/reshape | solution.py:58
  642.6 6.6 pad.8
  649.2 12.9 %reshape.154 = f32[200,32,289]{2,1,0:T(8,128)} reshape(f32[200,9248]{1,0:T(8,128)} %pad.8) | data formatting | bytes 14796800 | tf_op jit(solution)/shard_map/reshape | solution.py:59
  662.2 6.9 slice.51
  669.0 10.2 %reshape.151 = f32[200,9216]{1,0:T(8,128)} reshape(f32[200,32,288]{2,1,0:T(8,128)} %get-tuple-element.10) | data formatting | bytes 14745600 | tf_op jit(solution)/shard_map/reshape | solution.py:58
  679.3 6.6 pad.7
  685.9 12.9 %reshape.152 = f32[200,32,289]{2,1,0:T(8,128)} reshape(f32[200,9248]{1,0:T(8,128)} %pad.7) | data formatting | bytes 14796800 | tf_op jit(solution)/shard_map/reshape | solution.py:59
  698.8 6.8 slice.49
  705.6 17.1 %copy_bitcast_fusion = (f32[200,1,32,256]{3,0,1,2:T(8,128)}, f32[200,1,32,256]{3,0,1,2:T(8,128)}) fusion(f32[200,32,256]{2,1,0:T(8,128)} %slice.51, f32[200,32,256]{2,1,0:T(8,128)} %slice.49), kind=kLoop, calls=%fused_computation.5 | loop fusion | bytes 26214400 | tf_op jit(solution)/shard_map/stack | solution.py:70
  722.7 30.5 %fusion.5 = f32[32,256,256]{2,1,0:T(8,128)} fusion(f32[200,1,32,256]{3,0,1,2:T(8,128)} %get-tuple-element.18, f32[200,1,32,256]{3,0,1,2:T(8,128)} %get-tuple-element.19, f32[1,200,256]{2,1,0:T(8,128)S(1)} %get-tuple-element.15, f32[1,200,256]{2,1,0:T(8,128)S(1)} %get-tuple-element.14), kind=kOutput, calls=%fused_computation.9 | convolution fusion | flops 10069811200 | bytes 21905408 | tf_op jit(solution)/shard_map/bpco,pbm->com/dot_general | solution.py:91
  753.3 231.9 %reduce-scatter.2.cloned.1.call-done = f32[32,64,256]{2,1,0:T(8,128)} async-done(((f32[32,256,256]{2,1,0:T(8,128)}), f32[32,64,256]{2,1,0:T(8,128)}) %reduce-scatter.2.cloned.1.call-update) | async-done | bytes 2097168 | tf_op jit(solution)/shard_map/reduce_scatter | solution.py:92
  (23 shorter events, 5.6 us)
Async XLA Ops:
  17.9 60.4 %all-to-all-start = ((bf16[2,1000,1024]{1,0,2:T(2,128)(2,1)}), bf16[2,1000,1024]{1,0,2:T(2,128)(2,1)}, u32[]{:S(2)}, u32[]{:S(2)}) async-start(bf16[2,1000,1024]{1,0,2:T(2,128)(2,1)} %copy.11), calls=%async_computation | async-start | bytes 8388608 | tf_op jit(solution)/shard_map/all_to_all | solution.py:76
  28.2 956.9 %reduce-scatter.2.cloned.1.call-start = ((), (), s32[]{:S(2)}) async-start(), calls=%async_computation.2 | async-start | bytes 10485760 | tf_op jit(solution)/shard_map/reduce_scatter | solution.py:92
  106.9 80.7 %collective-permute-start = (bf16[400,64,32]{0,1,2:T(8,128)(2,1)S(1)}, bf16[400,64,32]{0,1,2:T(8,128)(2,1)S(1)}, u32[]{:S(2)}, u32[]{:S(2)}) collective-permute-start(bf16[400,64,32]{0,1,2:T(8,128)(2,1)S(1)} %get-tuple-element.6), channel_id=1, source_target_pairs={{4,0},{8,4},{12,8},{16,12},{20,16},{24,20},{28,24},{32,28},{36,32}... | collective-permute-start | bytes 4915208 | tf_op jit(solution)/shard_map/ppermute | solution.py:18
  111.4 154.9 %collective-permute-start.1 = (bf16[400,64,32]{0,1,2:T(8,128)(2,1)S(1)}, bf16[400,64,32]{0,1,2:T(8,128)(2,1)S(1)}, u32[]{:S(2)}, u32[]{:S(2)}) collective-permute-start(bf16[400,64,32]{0,1,2:T(8,128)(2,1)S(1)} %get-tuple-element.6), channel_id=1, source_target_pairs={{8,0},{12,4},{16,8},{20,12},{24,16},{28,20},{32,24},{36,28},{40,32... | collective-permute-start | bytes 4915208 | tf_op jit(solution)/shard_map/ppermute | solution.py:18
  117.9 218.4 %collective-permute-start.2 = (bf16[400,64,32]{0,1,2:T(8,128)(2,1)S(1)}, bf16[400,64,32]{0,1,2:T(8,128)(2,1)S(1)}, u32[]{:S(2)}, u32[]{:S(2)}) collective-permute-start(bf16[400,64,32]{0,1,2:T(8,128)(2,1)S(1)} %get-tuple-element.6), channel_id=1, source_target_pairs={{12,0},{16,4},{20,8},{24,12},{28,16},{32,20},{36,24},{40,28},{44,3... | collective-permute-start | bytes 4915208 | tf_op jit(solution)/shard_map/ppermute | solution.py:18
  121.3 304.6 %collective-permute-start.3 = (bf16[400,64,32]{0,1,2:T(8,128)(2,1)S(1)}, bf16[400,64,32]{0,1,2:T(8,128)(2,1)}, u32[]{:S(2)}, u32[]{:S(2)}) collective-permute-start(bf16[400,64,32]{0,1,2:T(8,128)(2,1)S(1)} %get-tuple-element.6), channel_id=1, source_target_pairs={{16,0},{20,4},{24,8},{28,12},{32,16},{36,20},{40,24},{44,28},{48,3... | collective-permute-start | bytes 4915208 | tf_op jit(solution)/shard_map/ppermute | solution.py:18
  124.3 304.7 %collective-permute-start.4 = (bf16[400,64,32]{0,1,2:T(8,128)(2,1)S(1)}, bf16[400,64,32]{0,1,2:T(8,128)(2,1)}, u32[]{:S(2)}, u32[]{:S(2)}) collective-permute-start(bf16[400,64,32]{0,1,2:T(8,128)(2,1)S(1)} %get-tuple-element.6), channel_id=1, source_target_pairs={{20,0},{24,4},{28,8},{32,12},{36,16},{40,20},{44,24},{48,28},{52,3... | collective-permute-start | bytes 4915208 | tf_op jit(solution)/shard_map/ppermute | solution.py:18
  187.6 1.4 copy-start.1
  189.0 243.2 %collective-permute-start.5 = (bf16[400,64,32]{0,1,2:T(8,128)(2,1)S(1)}, bf16[400,64,32]{0,1,2:T(8,128)(2,1)}, u32[]{:S(2)}, u32[]{:S(2)}) collective-permute-start(bf16[400,64,32]{0,1,2:T(8,128)(2,1)S(1)} %get-tuple-element.6), channel_id=1, source_target_pairs={{24,0},{28,4},{32,8},{36,12},{40,16},{44,20},{48,24},{52,28},{56,3... | collective-permute-start | bytes 4915208 | tf_op jit(solution)/shard_map/ppermute | solution.py:18
  266.3 71.9 %copy-start.2 = (bf16[400,64,32]{0,1,2:T(8,128)(2,1)}, bf16[400,64,32]{0,1,2:T(8,128)(2,1)S(1)}, u32[]{:S(2)}) copy-start(bf16[400,64,32]{0,1,2:T(8,128)(2,1)S(1)} %collective-permute-done.1) | copy-start | bytes 4915204
  266.3 176.6 %collective-permute-start.6 = (bf16[400,64,32]{0,1,2:T(8,128)(2,1)S(1)}, bf16[400,64,32]{0,1,2:T(8,128)(2,1)}, u32[]{:S(2)}, u32[]{:S(2)}) collective-permute-start(bf16[400,64,32]{0,1,2:T(8,128)(2,1)S(1)} %get-tuple-element.6), channel_id=1, source_target_pairs={{28,0},{32,4},{36,8},{40,12},{44,16},{48,20},{52,24},{56,28},{60,3... | collective-permute-start | bytes 4915208 | tf_op jit(solution)/shard_map/ppermute | solution.py:18
  336.3 2.0 copy-start.3
  336.3 151.6 %collective-permute-start.7 = (bf16[400,64,32]{0,1,2:T(8,128)(2,1)S(1)}, bf16[400,64,32]{0,1,2:T(8,128)(2,1)}, u32[]{:S(2)}, u32[]{:S(2)}) collective-permute-start(bf16[400,64,32]{0,1,2:T(8,128)(2,1)S(1)} %get-tuple-element.6), channel_id=1, source_target_pairs={{32,0},{36,4},{40,8},{44,12},{48,16},{52,20},{56,24},{60,28},{64,3... | collective-permute-start | bytes 4915208 | tf_op jit(solution)/shard_map/ppermute | solution.py:18
  345.8 6.5 copy-start.4
  552.0 44.7 %copy-start = (bf16[200,128,32]{1,2,0:T(8,128)(2,1)S(1)}, bf16[200,128,32]{1,2,0:T(8,128)(2,1)}, u32[]{:S(2)}) copy-start(bf16[200,128,32]{1,2,0:T(8,128)(2,1)} %copy.14) | copy-start | bytes 4915204
Sparse Core Ops, SparseCore 0:
  753.4 231.7 reduce-scatter.1
where the time goes:
time: 1000 us; the launch traced here: 992 us
  waiting for transfers between devices  536 us (54%)
  local copies, waits for them, and re-layouts  210 us (21%)
  starting transfers between devices  104 us (10%)
  other arithmetic  71 us (7%)
  matrix products  57.9 us (6%)
  between operations  14 us (1%)
    ppermute x8, waiting for transfers between devices, from_behind(): return lax.ppermute(block, axis, route)  258 us
    reduce_scatter x1, waiting for transfers between devices, per_device(): lax.psum_scatter(partial_sums, 'win', scatter_dimension=1, tiled=True)  232 us
    ppermute x8, starting transfers between devices, from_behind(): return lax.ppermute(block, axis, route)  93.3 us
    all_to_all x1, waiting for transfers between devices, per_device(): lax.all_to_all(records, 'chan', split_axis=2, concat_axis=0, tiled=True)  46.1 us
    concatenate x1, local copies, waits for them, and re-layouts, band_stack(): right_rows = jnp.concatenate([first, second], axis=2)  44.7 us
    concatenate x1, other arithmetic, band_stack(): right_rows = jnp.concatenate([first, second], axis=2)  42.1 us
    unnamed x18, local copies, waits for them, and re-layouts  33.4 us
    dot_general x1, matrix products, per_device(): jnp.einsum('bpco,pbm->com', stacks, lag_table, precision=lax.Precision.HI...  30.5 us
  transfers between devices with their start and end apart: 10, of which 7 were waited for; matrix products, arithmetic and copies ran while one was open for 3% of the time, Pallas kernels for 0%

commit v1 on v0

v1 whole, which is shorter than its diff:
```python
import functools
import math

import jax
import jax.numpy as jnp
import ml_dtypes
import numpy as np
from jax import lax
from jax.experimental import pallas as pl
from jax.experimental.pallas import tpu as pltpu
from jax.sharding import PartitionSpec as P

SAMPLES = 1000
BINS = 200
FIRST_BIN = 20
BAND = 256
LAGS = 256
WINDOWS = 256
PER_DEVICE = 2
OWNERS = BINS // PER_DEVICE
OWNER_ROWS = 104
PART_ROWS = PER_DEVICE * OWNER_ROWS
VMEM_LIMIT = 50 * 1024 * 1024


def bins_of_rows():
    rows = np.arange(PART_ROWS)
    owner = rows % OWNER_ROWS
    return np.where(owner < OWNERS, owner * PER_DEVICE + rows // OWNER_ROWS, -1)


def dft_rows():
    bins = bins_of_rows()
    turns = (FIRST_BIN + np.maximum(bins, 0))[:, None] * np.arange(SAMPLES)[None, :] % SAMPLES
    phase = turns * (2.0 * math.pi / SAMPLES)
    both = np.concatenate([np.cos(phase), -np.sin(phase)], axis=0)
    valid = np.concatenate([bins, bins]) >= 0
    return np.where(valid[:, None], both, 0.0).astype(ml_dtypes.bfloat16)


def box_rows():
    bins = bins_of_rows()
    valid = bins >= 0
    near = (np.abs(bins[:, None] - bins[None, :]) <= 4) & valid[:, None] & valid[None, :]
    count = np.maximum(near.sum(axis=1, keepdims=True), 1)
    return near.astype(ml_dtypes.bfloat16), (1.0 / count).astype(np.float32)


def lag_rows():
    freqs = FIRST_BIN + np.arange(BINS)
    shifts = np.arange(LAGS) - LAGS // 2
    phase = (freqs[:, None] * shifts[None, :] % SAMPLES) * (2.0 * math.pi / SAMPLES)
    table = np.stack([np.cos(phase), -np.sin(phase)], axis=1) / (WINDOWS * math.sqrt(BINS))
    table = table.reshape(2 * BINS, LAGS)
    high = table.astype(ml_dtypes.bfloat16)
    low = (table - high.astype(np.float64)).astype(ml_dtypes.bfloat16)
    return np.concatenate([high, low], axis=1)


def dot(left, right, left_dim, right_dim):
    dims = (((left_dim,), (right_dim,)), ((), ()))
    return lax.dot_general(left, right, dims, preferred_element_type=jnp.float32)


def whiten_kernel(records_ref, dft_ref, box_ref, weight_ref, out_ref, rows_ref):
    windows = records_ref.shape[0]
    rows_ref[...] = jnp.zeros_like(rows_ref)
    blocks = rows_ref.shape[0]
    for w in range(windows):
        spectra = dot(dft_ref[...], records_ref[w], 1, 0)
        real_part = spectra[:PART_ROWS]
        imag_part = spectra[PART_ROWS:]
        power = real_part * real_part + imag_part * imag_part
        size = jnp.sqrt(power)
        high = size.astype(jnp.bfloat16)
        low = (size - high.astype(jnp.float32)).astype(jnp.bfloat16)
        smooth = (dot(box_ref[...], high, 1, 0) + dot(box_ref[...], low, 1, 0)) * weight_ref[...]
        level = jnp.sqrt(jnp.sum(power, axis=0, keepdims=True) * (1.0 / BINS) + 1e-06)
        scale = 1.0 / (smooth + 0.25 * level)
        for part, values in enumerate((real_part * scale, imag_part * scale)):
            for b in range(PER_DEVICE):
                piece = values[b * OWNER_ROWS : (b + 1) * OWNER_ROWS]
                place = (part * windows + w) * PER_DEVICE + b
                for n in range(blocks):
                    rows_ref[n, pl.ds(place, OWNER_ROWS, stride=8), :] = piece[:, n * 128 : (n + 1) * 128]
    for n in range(blocks):
        out_ref[:, n * 128 : (n + 1) * 128] = rows_ref[n].astype(jnp.bfloat16)


def whiten(records, devices):
    windows, samples, channels = records.shape
    block = 512
    near, weight = box_rows()
    rows = devices * windows * 2 * PER_DEVICE
    whole = lambda shape: pl.BlockSpec(shape, lambda i: (0, 0))
    return pl.pallas_call(
        whiten_kernel,
        grid=(channels // block,),
        in_specs=[
            pl.BlockSpec((windows, samples, block), lambda i: (0, 0, i)),
            whole((2 * PART_ROWS, samples)),
            whole((PART_ROWS, PART_ROWS)),
            whole((PART_ROWS, 1)),
        ],
        out_specs=pl.BlockSpec((rows, block), lambda i: (0, i)),
        out_shape=jax.ShapeDtypeStruct((rows, channels), jnp.bfloat16),
        scratch_shapes=[pltpu.VMEM((block // 128, rows, 128), jnp.float32)],
        compiler_params=pltpu.CompilerParams(vmem_limit_bytes=VMEM_LIMIT),
        name="whiten",
    )(records, jnp.asarray(dft_rows()), jnp.asarray(near), jnp.asarray(weight))


def stack_kernel(rows_ref, flip_ref, out_ref):
    row_count, channels = rows_ref.shape
    block = flip_ref.shape[0]
    row = lax.broadcasted_iota(jnp.int32, (1, 8, block), 1)
    sign = jnp.where(row < 4, 1.0, -1.0)
    column = lax.broadcasted_iota(jnp.int32, (1, row_count), 1)
    lane = lax.broadcasted_iota(jnp.int32, (8, 16, 128), 2)
    for c in range(channels // block):
        begin = c * block
        extent = min(2 * block, channels - begin)
        plain = rows_ref[:, begin : begin + block]
        turned = plain.astype(jnp.float32).reshape(row_count // 8, 8, block)
        turned = (pltpu.roll(turned, 4, 1) * sign).reshape(row_count, block).astype(jnp.bfloat16)
        flipped = [dot(flip_ref[...], side, 1, 1) for side in (plain, turned)]
        sides = []
        for b in range(PER_DEVICE):
            keep = jnp.where(column % PER_DEVICE == b, 1.0, 0.0)
            sides += [(side * keep).astype(jnp.bfloat16) for side in flipped]
        left = jnp.concatenate(sides, axis=0)
        products = dot(left, rows_ref[:, begin : begin + extent], 1, 0)
        for p in range(2 * PER_DEVICE):
            product = products[p * block : (p + 1) * block]
            if extent < 2 * block:
                product = jnp.concatenate([product, jnp.zeros_like(product)], axis=1)
            skewed = pltpu.roll(product, block + 1, 1, stride=1, stride_axis=0)[:, :BAND]
            halves = skewed.reshape(8, 2, 16, BAND)
            for q in range(BAND // 128):
                first = halves[:, 1, :, q * 128 : (q + 1) * 128]
                second = halves[:, 0, :, q * 128 : (q + 1) * 128]
                even = jnp.where(lane < 64, first, pltpu.roll(second, 64, 2)).astype(jnp.bfloat16)
                odd = jnp.where(lane < 64, pltpu.roll(first, 64, 2), second).astype(jnp.bfloat16)
                for i in range(8):
                    out_ref[c * 8 + 7 - i, 2 * q, p * 16 : (p + 1) * 16, :] = even[i]
                    out_ref[c * 8 + 7 - i, 2 * q + 1, p * 16 : (p + 1) * 16, :] = odd[i]


def stack(rows, chan_size, win_size):
    return pl.pallas_call(
        stack_kernel,
        out_shape=jax.ShapeDtypeStruct((chan_size, win_size, 64, 128), jnp.bfloat16),
        in_specs=[pl.BlockSpec(memory_space=pltpu.VMEM)] * 2,
        out_specs=pl.BlockSpec(memory_space=pltpu.VMEM),
        compiler_params=pltpu.CompilerParams(vmem_limit_bytes=VMEM_LIMIT),
        name="stack",
    )(rows, jnp.asarray(np.eye(256)[::-1], jnp.bfloat16))


def lag_kernel(stacks_ref, table_ref, out_ref, wide_ref):
    step = pl.program_id(0)

    @pl.when(step == 0)
    def _():
        wide_ref[...] = stacks_ref[...].astype(jnp.float32)

    left = wide_ref[pl.ds(15 - step, 2 * BINS, stride=16), :].astype(jnp.bfloat16)
    both = dot(left, table_ref[...], 0, 0)
    lags = both[:, :LAGS] + both[:, LAGS:]
    out_ref[...] = lags.reshape(2, 1, 64, LAGS)


def lag_transform(stacks):
    used = 2 * BINS * 16
    out = pl.pallas_call(
        lag_kernel,
        grid=(16,),
        in_specs=[
            pl.BlockSpec((used, 128), lambda i: (0, 0)),
            pl.BlockSpec((2 * BINS, 2 * LAGS), lambda i: (0, 0)),
        ],
        out_specs=pl.BlockSpec((2, 1, 64, LAGS), lambda i: (0, i, 0, 0)),
        out_shape=jax.ShapeDtypeStruct((2, 16, 64, LAGS), jnp.float32),
        scratch_shapes=[pltpu.VMEM((used, 128), jnp.float32)],
        compiler_params=pltpu.CompilerParams(vmem_limit_bytes=VMEM_LIMIT),
        name="lag_transform",
    )(stacks, jnp.asarray(lag_rows()))
    return out.reshape(32, 64, LAGS)


def per_device(chan_size, win_size, records):
    devices = chan_size * win_size
    axes = ("chan", "win")
    channels = records.shape[2]
    rows = whiten(records, devices).reshape(devices, 8, channels)
    rows = lax.all_to_all(rows, axes, split_axis=0, concat_axis=0, tiled=True)
    stacks = stack(rows.reshape(devices * 8, channels), chan_size, win_size)
    stacks = stacks.reshape(devices, 64, 128)
    stacks = lax.all_to_all(stacks, axes, split_axis=0, concat_axis=0, tiled=True)
    return lag_transform(stacks.reshape(devices * 64, 128))


def solution(mesh):
    in_specs = (P(("chan", "win"), None, None),)
    out_specs = P("chan", "win", None)
    body = functools.partial(per_device, mesh.shape["chan"], mesh.shape["win"])
    return jax.shard_map(body, mesh=mesh, in_specs=in_specs, out_specs=out_specs, check_vma=False)
```

time: 1000 us -> 104 us (0.10)
  the two profiles are of different devices: /device:TPU:21 before, /device:TPU:1 now
where the time goes in v1:
time: 104 us; the launch traced here: 103 us
  blocking collectives  76.1 us (73%)
  Pallas kernels  24.4 us (23%)
  local copies, waits for them, and re-layouts  2.96 us (3%)
    all_to_all x1, blocking collectives, per_device(): rows = lax.all_to_all(rows, axes, split_axis=0, concat_axis=0, tiled=True)  41.4 us
    all_to_all x1, blocking collectives, per_device(): lax.all_to_all(stacks, axes, split_axis=0, concat_axis=0, tiled=True)  34.6 us
    pallas_call x1, Pallas kernels, stack(): pl.pallas_call(stack_kernel, out_shape=jax.ShapeDtypeStruct((chan_size, w...  9.57 us
    pallas_call x1, Pallas kernels, lag_transform(): pl.pallas_call(lag_kernel, grid=(16,), in_specs=[pl.BlockSpec((used, 128)...  8.69 us
    pallas_call x1, Pallas kernels, whiten(): pl.pallas_call(whiten_kernel, grid=(channels // block,), in_specs=[pl.Blo...  6.16 us
    unnamed x10, local copies, waits for them, and re-layouts  2.96 us

profile of v1, /device:TPU:1, one launch (start us, length us, event | category | flops | bytes accessed | tf_op | source)
XLA Modules:
  0.0 103.5 jit_solution(6387579454359807757)
XLA Ops:
  0.0 0.0 copy-start
  0.0 1.2 %copy-done = bf16[416,1000]{1,0:T(8,128)(2,1)S(1)} copy-done((bf16[416,1000]{1,0:T(8,128)(2,1)S(1)}, bf16[416,1000]{1,0:T(8,128)(2,1)}, u32[]{:S(2)}) %copy-start) | copy-done | bytes 832024
  1.2 0.0 copy-start.3
  1.2 0.9 copy-done.3
  2.1 0.0 copy-start.4
  2.1 0.9 copy-done.4
  2.9 6.2 %whiten.1 = bf16[1024,1024]{1,0:T(8,128)(2,1)S(1)} custom-call(bf16[2,1000,1024]{2,1,0:T(8,128)(2,1)} %records_ref.1, bf16[416,1000]{1,0:T(8,128)(2,1)S(1)} %copy-done, bf16[208,208]{1,0:T(8,128)(2,1)S(1)} %copy-done.4, f32[208,1]{1,0:T(8,128)S(1)} %copy-done.3), custom_call_target="tpu_custom_call" | custom-call | tf_op jit(solution)/shard_map/whiten/pallas_call | solution.py:96
  9.1 0.0 copy-start.2
  9.1 41.4 %all_to_all.10 = bf16[128,8,1024]{2,1,0:T(8,128)(2,1)} all-to-all(bf16[128,8,1024]{2,1,0:T(8,128)(2,1)S(1)} %bitcast.5), channel_id=1, replica_groups=mesh['chan'=32,'win'=4] {'chan','win'}, dimensions={0} | all-to-all | bytes 4194304 | tf_op jit(solution)/shard_map/all_to_all | solution.py:196
  50.6 0.0 copy-done.2
  50.6 9.6 %stack.1 = bf16[32,4,64,128]{3,2,1,0:T(8,128)(2,1)S(1)} custom-call(bf16[1024,1024]{1,0:T(8,128)(2,1)} %bitcast.8, bf16[256,256]{1,0:T(8,128)(2,1)S(1)} %copy-done.2), custom_call_target="tpu_custom_call" | custom-call | tf_op jit(solution)/shard_map/stack/pallas_call | solution.py:150
  60.2 0.0 copy-start.1
  60.2 34.6 %all_to_all.11 = bf16[128,64,128]{2,1,0:T(8,128)(2,1)S(1)} all-to-all(bf16[128,64,128]{2,1,0:T(8,128)(2,1)S(1)} %bitcast.6), channel_id=1, replica_groups=mesh['chan'=32,'win'=4] {'chan','win'}, dimensions={0} | all-to-all | bytes 4194304 | tf_op jit(solution)/shard_map/all_to_all | solution.py:199
  94.8 0.0 copy-done.1
  94.8 8.7 %lag_transform.1 = f32[2,16,64,256]{3,2,1,0:T(8,128)} custom-call(bf16[8192,128]{1,0:T(8,128)(2,1)S(1)} %bitcast.7, bf16[400,512]{1,0:T(8,128)(2,1)S(1)} %copy-done.1), custom_call_target="tpu_custom_call" | custom-call | tf_op jit(solution)/shard_map/lag_transform/pallas_call | solution.py:175
Async XLA Ops:
  0.0 1.2 %copy-start = (bf16[416,1000]{1,0:T(8,128)(2,1)S(1)}, bf16[416,1000]{1,0:T(8,128)(2,1)}, u32[]{:S(2)}) copy-start(bf16[416,1000]{1,0:T(8,128)(2,1)} %constant.10.clone.dft_ref) | copy-start | bytes 2496004
  1.2 0.9 copy-start.3
  2.1 0.9 copy-start.4
  9.1 41.5 %copy-start.2 = (bf16[256,256]{1,0:T(8,128)(2,1)S(1)}, bf16[256,256]{1,0:T(8,128)(2,1)}, u32[]{:S(2)}) copy-start(bf16[256,256]{1,0:T(8,128)(2,1)} %constant.13.clone.flip_ref) | copy-start | bytes 393220
  60.2 34.6 %copy-start.1 = (bf16[400,512]{1,0:T(8,128)(2,1)S(1)}, bf16[400,512]{1,0:T(8,128)(2,1)}, u32[]{:S(2)}) copy-start(bf16[400,512]{1,0:T(8,128)(2,1)} %constant.14.clone.table_ref) | copy-start | bytes 1228804

commit v2 on v1

v2 whole, which is shorter than its diff:
```python
import functools
import math

import jax
import jax.numpy as jnp
import ml_dtypes
import numpy as np
from jax import lax
from jax.experimental import pallas as pl
from jax.experimental.pallas import tpu as pltpu
from jax.sharding import PartitionSpec as P

SAMPLES = 1000
BINS = 200
FIRST_BIN = 20
BAND = 256
LAGS = 256
WINDOWS = 256
OWNERS = BINS // 2
OWNER_ROWS = 104
ROWS = 2 * OWNER_ROWS
VMEM_LIMIT = 50 * 1024 * 1024


def dft_rows():
    turns = (FIRST_BIN + np.arange(BINS))[:, None] * np.arange(SAMPLES)[None, :] % SAMPLES
    phase = turns * (2.0 * math.pi / SAMPLES)
    table = np.stack([np.cos(phase), -np.sin(phase)]).reshape(4, OWNERS, SAMPLES)
    table = np.pad(table, ((0, 0), (0, OWNER_ROWS - OWNERS), (0, 0)))
    return table.reshape(4 * OWNER_ROWS, SAMPLES).astype(ml_dtypes.bfloat16)


def lag_rows():
    shifts = np.arange(LAGS) - LAGS // 2
    bins = np.arange(BINS).reshape(2, OWNERS).T.reshape(-1)
    phase = ((FIRST_BIN + bins)[:, None] * shifts[None, :] % SAMPLES) * (2.0 * math.pi / SAMPLES)
    table = np.stack([np.cos(phase), -np.sin(phase)], axis=1) / (WINDOWS * math.sqrt(BINS))
    table = table.reshape(2 * BINS, LAGS)
    high = table.astype(ml_dtypes.bfloat16)
    low = (table - high.astype(np.float64)).astype(ml_dtypes.bfloat16)
    return np.concatenate([high, low], axis=1)


def dot(left, right, left_dim, right_dim):
    dims = (((left_dim,), (right_dim,)), ((), ()))
    return lax.dot_general(left, right, dims, preferred_element_type=jnp.float32)


def params():
    return pltpu.CompilerParams(vmem_limit_bytes=VMEM_LIMIT)


def cost(flops, bytes_accessed):
    return pl.CostEstimate(flops=flops, bytes_accessed=bytes_accessed, transcendentals=0)


def bin_of(row):
    return jnp.where(row < OWNER_ROWS, row, row - (OWNER_ROWS - OWNERS))


def near_matrix():
    row = lax.broadcasted_iota(jnp.int32, (ROWS, ROWS), 0)
    column = lax.broadcasted_iota(jnp.int32, (ROWS, ROWS), 1)
    near = jnp.abs(bin_of(row) - bin_of(column)) <= 4
    near = near & (row % OWNER_ROWS < OWNERS) & (column % OWNER_ROWS < OWNERS)
    return jnp.where(near, 1.0, 0.0).astype(jnp.bfloat16)


def whiten_kernel(records_ref, dft_ref, out_ref, rows_ref):
    windows = records_ref.shape[0]
    blocks, row_count, _ = rows_ref.shape
    near = near_matrix()
    place = bin_of(lax.broadcasted_iota(jnp.int32, (ROWS, 1), 0))
    count = jnp.minimum(place + 4, BINS - 1) - jnp.maximum(place - 4, 0) + 1
    weight = 1.0 / count.astype(jnp.float32)

    @pl.when(pl.program_id(0) == 0)
    def _():
        rest = row_count - OWNER_ROWS * 8
        rows_ref[:, OWNER_ROWS * 8 :, :] = jnp.zeros((blocks, rest, 128), jnp.float32)

    for w in range(windows):
        spectra = dot(dft_ref[...], records_ref[w], 1, 0)
        real_part = spectra[:ROWS]
        imag_part = spectra[ROWS:]
        power = real_part * real_part + imag_part * imag_part
        size = jnp.sqrt(power)
        high = size.astype(jnp.bfloat16)
        low = (size - high.astype(jnp.float32)).astype(jnp.bfloat16)
        smooth = (dot(near, high, 1, 0) + dot(near, low, 1, 0)) * weight
        level = jnp.sqrt(jnp.sum(power, axis=0, keepdims=True) * (1.0 / BINS) + 1e-06)
        scale = 1.0 / (smooth + 0.25 * level)
        for part, values in enumerate((real_part * scale, imag_part * scale)):
            place = part * windows + w
            for n in range(blocks):
                piece = values[:, n * 128 : (n + 1) * 128]
                for b in range(2):
                    rows_ref[n, pl.ds(b * 4 + place, OWNER_ROWS, stride=8), :] = piece[
                        b * OWNER_ROWS : (b + 1) * OWNER_ROWS
                    ]
    for n in range(blocks):
        out_ref[:, n * 128 : (n + 1) * 128] = rows_ref[n].astype(jnp.bfloat16)


def whiten(records, devices):
    windows, samples, channels = records.shape
    rows = devices * 8
    block = 512
    return pl.pallas_call(
        whiten_kernel,
        grid=(channels // block,),
        in_specs=[
            pl.BlockSpec((windows, samples, block), lambda i: (0, 0, i)),
            pl.BlockSpec((2 * ROWS, samples), lambda i: (0, 0)),
        ],
        out_specs=pl.BlockSpec((rows, block), lambda i: (0, i)),
        out_shape=jax.ShapeDtypeStruct((rows, channels), jnp.bfloat16),
        scratch_shapes=[pltpu.VMEM((block // 128, rows, 128), jnp.float32)],
        compiler_params=params(),
        cost_estimate=cost(2 * windows * samples * channels * 2 * BINS, records.size * 2 + rows * channels * 2),
        name="whiten",
    )(records, jnp.asarray(dft_rows()))


def stack_kernel(rows_ref, out_ref, plain_ref, turned_ref):
    row_count, channels = rows_ref.shape
    block = 256
    row = lax.broadcasted_iota(jnp.int32, (1, 8, block), 1)
    for begin in range(0, channels, block):
        wide = rows_ref[:, begin : begin + block].astype(jnp.float32).reshape(row_count // 16, 2, 8, block)
        even, odd = wide[:, 0], wide[:, 1]
        halves = (
            jnp.where(row < 4, even, pltpu.roll(odd, 4, 1)),
            jnp.where(row < 4, pltpu.roll(even, 4, 1), odd),
        )
        for b, half in enumerate(halves):
            turned = jnp.where(row // 2 % 2 == 0, pltpu.roll(half, 6, 1), -pltpu.roll(half, 2, 1))
            for ref, value in ((plain_ref, half), (turned_ref, turned)):
                ref[b, :, begin : begin + block] = value.reshape(row_count // 2, block).astype(jnp.bfloat16)
    row = lax.broadcasted_iota(jnp.int32, (block, block), 0)
    column = lax.broadcasted_iota(jnp.int32, (block, block), 1)
    flip = jnp.where(row + column == block - 1, 1.0, 0.0).astype(jnp.bfloat16)
    lane = lax.broadcasted_iota(jnp.int32, (16, 128), 1)
    for b in range(2):
        for c in range(channels // block):
            begin = c * block
            sides = [dot(flip, ref[b, :, begin : begin + block], 1, 1) for ref in (plain_ref, turned_ref)]
            sides = [side.astype(jnp.bfloat16) for side in sides]
            for u in range(2):
                left = jnp.concatenate([side[u * 128 : (u + 1) * 128] for side in sides], axis=0)
                right = begin + 128 * (1 - u)
                extent = min(384, channels - right)
                products = dot(left, plain_ref[b, :, right : right + extent], 1, 0)
                if extent < 384:
                    products = jnp.concatenate([products, jnp.zeros((256, 384 - extent), jnp.float32)], axis=1)
                for p in range(2):
                    item = (b * 2 + p) * 16
                    for i in range(4):
                        r = p * 128 + i * 32
                        second = pltpu.roll(products[r : r + 16], (321 + 32 * i) % 384, 1, stride=1, stride_axis=0)
                        first = pltpu.roll(products[r + 16 : r + 32], (273 + 32 * i) % 384, 1, stride=1, stride_axis=0)
                        where = c * 8 + 7 - u * 4 - i
                        for q in range(2):
                            now = slice(q * 128, (q + 1) * 128)
                            then = slice((q + 1) * 128, (q + 2) * 128)
                            low = jnp.where(lane < 64, first[:, now], second[:, now])
                            high = jnp.where(lane < 64, second[:, then], first[:, now])
                            out_ref[where, 2 * q, item : item + 16, :] = low.astype(jnp.bfloat16)
                            out_ref[where, 2 * q + 1, item : item + 16, :] = high.astype(jnp.bfloat16)


def stack(rows, chan_size, win_size):
    row_count, channels = rows.shape
    return pl.pallas_call(
        stack_kernel,
        out_shape=jax.ShapeDtypeStruct((chan_size, win_size, 64, 128), jnp.bfloat16),
        in_specs=[pl.BlockSpec(memory_space=pltpu.VMEM)],
        out_specs=pl.BlockSpec(memory_space=pltpu.VMEM),
        scratch_shapes=[pltpu.VMEM((2, row_count // 2, channels), jnp.bfloat16)] * 2,
        compiler_params=params(),
        cost_estimate=cost(4 * 2 * 1024 * 512 * 512, 4 * 1024 * 1024),
        name="stack",
    )(rows)


def lag_kernel(steps, swap_ref, table_ref, stacks_ref, out_ref, wide_ref):
    step = pl.program_id(0)
    items = table_ref.shape[0]
    each = 16 // steps

    @pl.when(step == 0)
    def _():
        wide_ref[...] = stacks_ref[...].astype(jnp.float32)

    sides = []
    for n in range(each):
        place = 15 - (step * each + n)
        sides.append(wide_ref[pl.ds(place, items, stride=16), :].astype(jnp.bfloat16))
    both = dot(jnp.concatenate(sides, axis=1), table_ref[...], 0, 0)
    lags = both[:, :LAGS] + both[:, LAGS:]
    swap = swap_ref[0]
    for n in range(each):
        for h in range(2):
            r = n * 128 + h * 64
            out_ref[(h + swap) % 2, n] = lags[r : r + 64]


def lag_transform(stacks, swap):
    steps = 4
    table = jnp.asarray(lag_rows())
    rows = 2 * BINS * 16
    out = pl.pallas_call(
        functools.partial(lag_kernel, steps),
        grid=(steps,),
        in_specs=[
            pl.BlockSpec(memory_space=pltpu.SMEM),
            pl.BlockSpec(table.shape, lambda i: (0, 0)),
            pl.BlockSpec((rows, 128), lambda i: (0, 0)),
        ],
        out_specs=pl.BlockSpec((2, 16 // steps, 64, LAGS), lambda i: (0, i, 0, 0)),
        out_shape=jax.ShapeDtypeStruct((2, 16, 64, LAGS), jnp.float32),
        scratch_shapes=[pltpu.VMEM((rows, 128), jnp.float32)],
        compiler_params=params(),
        cost_estimate=cost(4 * 2 * BINS * 2048 * 256, 4 * 1024 * 1024),
        name="lag_transform",
    )(swap, table, stacks)
    return out.reshape(32, 64, LAGS)


def per_device(chan_size, win_size, records):
    devices = chan_size * win_size
    axes = ("chan", "win")
    channels = records.shape[2]
    rows = whiten(records, devices).reshape(devices, 8, channels)
    rows = lax.all_to_all(rows, axes, split_axis=0, concat_axis=0, tiled=True)
    stacks = stack(rows.reshape(devices * 8, channels), chan_size, win_size)
    stacks = stacks.reshape(devices, 64, 128)
    stacks = lax.all_to_all(stacks, axes, split_axis=0, concat_axis=0, tiled=True)
    swap = jnp.full((1,), lax.axis_index("win") % 2, jnp.int32)
    return lag_transform(stacks.reshape(devices * 64, 128), swap)


def solution(mesh):
    in_specs = (P(("chan", "win"), None, None),)
    out_specs = P("chan", "win", None)
    body = functools.partial(per_device, mesh.shape["chan"], mesh.shape["win"])
    return jax.shard_map(body, mesh=mesh, in_specs=in_specs, out_specs=out_specs, check_vma=False)
```

time: 104 us -> 95.8 us (0.921)
  blocking collectives: 76.1 us -> 41.4 us
  waiting for transfers between devices: 0 us -> 30.2 us
  Pallas kernels: 24.4 us -> 16.6 us
  starting transfers between devices: 0 us -> 4.89 us
    all_to_all x1 -> x0, blocking collectives: 34.6 us -> none  [per_device(): lax.all_to_all(stacks, axes, split_axis=0, concat_axis=0, tiled=True)]
    all_to_all x0 -> x1, waiting for transfers between devices: none -> 30.2 us  [per_device(): lax.all_to_all(stacks, axes, split_axis=0, concat_axis=0, tiled=True)]
    all_to_all x0 -> x1, starting transfers between devices: none -> 4.89 us  [per_device(): lax.all_to_all(stacks, axes, split_axis=0, concat_axis=0, tiled=True)]
    pallas_call x1, Pallas kernels: 8.69 us -> 4.34 us  [lag_transform(): pl.pallas_call(functools.partial(lag_kernel, steps), grid=(steps,), in_sp...]
    pallas_call x1, Pallas kernels: 9.57 us -> 5.92 us  [stack(): pl.pallas_call(stack_kernel, out_shape=jax.ShapeDtypeStruct((chan_size, w...]
    unnamed x10 -> x6, local copies, waits for them, and re-layouts: 2.96 us -> 2.47 us
  transfers between devices with their start and end apart: 0 -> 1, of which waited for: 0 -> 1; matrix products, arithmetic and copies ran while one was open for 0% -> 0% of each run, Pallas kernels for 0% -> 0%
where the time goes in v2:
time: 95.8 us; the launch traced here: 95.6 us
  blocking collectives  41.4 us (43%)
  waiting for transfers between devices  30.2 us (32%)
  Pallas kernels  16.6 us (17%)
  starting transfers between devices  4.89 us (5%)
  local copies, waits for them, and re-layouts  2.47 us (3%)
    all_to_all x1, blocking collectives, per_device(): rows = lax.all_to_all(rows, axes, split_axis=0, concat_axis=0, tiled=True)  41.4 us
    all_to_all x1, waiting for transfers between devices, per_device(): lax.all_to_all(stacks, axes, split_axis=0, concat_axis=0, tiled=True)  30.2 us
    pallas_call x1, Pallas kernels, whiten(): pl.pallas_call(whiten_kernel, grid=(channels // block,), in_specs=[pl.Blo...  6.32 us
    pallas_call x1, Pallas kernels, stack(): pl.pallas_call(stack_kernel, out_shape=jax.ShapeDtypeStruct((chan_size, w...  5.92 us
    all_to_all x1, starting transfers between devices, per_device(): lax.all_to_all(stacks, axes, split_axis=0, concat_axis=0, tiled=True)  4.89 us
    pallas_call x1, Pallas kernels, lag_transform(): pl.pallas_call(functools.partial(lag_kernel, steps), grid=(steps,), in_sp...  4.34 us
    unnamed x6, local copies, waits for them, and re-layouts  2.47 us
  transfers between devices with their start and end apart: 1, of which 1 were waited for; matrix products, arithmetic and copies ran while one was open for 0% of the time, Pallas kernels for 0%

profile of v2, /device:TPU:1, one launch (start us, length us, event | category | flops | bytes accessed | tf_op | source)
XLA Modules:
  0.0 95.6 jit_solution(16500856743612634049)
XLA Ops:
  0.0 0.0 copy-start.1
  0.0 1.2 %copy-done.1 = bf16[416,1000]{1,0:T(8,128)(2,1)S(1)} copy-done((bf16[416,1000]{1,0:T(8,128)(2,1)S(1)}, bf16[416,1000]{1,0:T(8,128)(2,1)}, u32[]{:S(2)}) %copy-start.1) | copy-done | bytes 832024
  1.2 6.3 %whiten.1 = bf16[1024,1024]{1,0:T(8,128)(2,1)S(1)} custom-call(bf16[2,1000,1024]{2,1,0:T(8,128)(2,1)} %records_ref.1, bf16[416,1000]{1,0:T(8,128)(2,1)S(1)} %copy-done.1), custom_call_target="tpu_custom_call" | custom-call | flops 1638400000 | bytes 6193152 | tf_op jit(solution)/shard_map/whiten/pallas_call | solution.py:109
  7.5 41.4 %all_to_all.10 = bf16[128,8,1024]{2,1,0:T(8,128)(2,1)} all-to-all(bf16[128,8,1024]{2,1,0:T(8,128)(2,1)S(1)} %bitcast.6), channel_id=1, replica_groups=mesh['chan'=32,'win'=4] {'chan','win'}, dimensions={0} | all-to-all | bytes 4194304 | tf_op jit(solution)/shard_map/all_to_all | solution.py:235
  48.9 5.9 %stack.1 = bf16[32,4,64,128]{3,2,1,0:T(8,128)(2,1)S(1)} custom-call(bf16[1024,1024]{1,0:T(8,128)(2,1)} %bitcast.9), custom_call_target="tpu_custom_call" | custom-call | flops 2147483648 | bytes 4194304 | tf_op jit(solution)/shard_map/stack/pallas_call | solution.py:174
  54.8 0.0 copy-start
  54.9 1.3 %copy-done = bf16[32,4,64,128]{3,2,1,0:T(8,128)(2,1)} copy-done((bf16[32,4,64,128]{3,2,1,0:T(8,128)(2,1)}, bf16[32,4,64,128]{3,2,1,0:T(8,128)(2,1)S(1)}, u32[]{:S(2)}) %copy-start) | copy-done | bytes 2097176
  56.2 0.0 copy-start.2
  56.2 4.9 %all-to-all-start.1 = ((bf16[128,64,128]{2,1,0:T(8,128)(2,1)}), bf16[128,64,128]{2,1,0:T(8,128)(2,1)S(1)}, u32[]{:S(2)}, u32[]{:S(2)}) async-start(bf16[128,64,128]{2,1,0:T(8,128)(2,1)} %bitcast.8), calls=%async_computation.1 | async-start | bytes 4194304 | tf_op jit(solution)/shard_map/all_to_all | solution.py:238
  61.1 30.2 %all-to-all-done.1 = bf16[128,64,128]{2,1,0:T(8,128)(2,1)S(1)} async-done(((bf16[128,64,128]{2,1,0:T(8,128)(2,1)}), bf16[128,64,128]{2,1,0:T(8,128)(2,1)S(1)}, u32[]{:S(2)}, u32[]{:S(2)}) %all-to-all-start.1) | async-done | bytes 2097184 | tf_op jit(solution)/shard_map/all_to_all | solution.py:238
  91.2 0.0 copy-done.2
  91.2 4.3 %lag_transform.1 = f32[2,16,64,256]{3,2,1,0:T(8,128)} custom-call(s32[1]{0:T(128)} %bitcast.swap_ref, bf16[400,512]{1,0:T(8,128)(2,1)S(1)} %copy-done.2, bf16[8192,128]{1,0:T(8,128)(2,1)S(1)} %bitcast.7), custom_call_target="tpu_custom_call" | custom-call | flops 838860800 | bytes 4194304 | tf_op jit(solution)/shard_map/lag_transform/pallas_call | solution.py:212
Async XLA Ops:
  0.0 1.2 %copy-start.1 = (bf16[416,1000]{1,0:T(8,128)(2,1)S(1)}, bf16[416,1000]{1,0:T(8,128)(2,1)}, u32[]{:S(2)}) copy-start(bf16[416,1000]{1,0:T(8,128)(2,1)} %constant.21.clone.dft_ref) | copy-start | bytes 2496004
  54.8 1.3 %copy-start = (bf16[32,4,64,128]{3,2,1,0:T(8,128)(2,1)}, bf16[32,4,64,128]{3,2,1,0:T(8,128)(2,1)S(1)}, u32[]{:S(2)}) copy-start(bf16[32,4,64,128]{3,2,1,0:T(8,128)(2,1)S(1)} %stack.1) | copy-start | bytes 6291460
  56.2 35.1 %copy-start.2 = (bf16[400,512]{1,0:T(8,128)(2,1)S(1)}, bf16[400,512]{1,0:T(8,128)(2,1)}, u32[]{:S(2)}) copy-start(bf16[400,512]{1,0:T(8,128)(2,1)} %constant.22.clone.table_ref) | copy-start | bytes 1228804
  56.2 35.1 %all-to-all-start.1 = ((bf16[128,64,128]{2,1,0:T(8,128)(2,1)}), bf16[128,64,128]{2,1,0:T(8,128)(2,1)S(1)}, u32[]{:S(2)}, u32[]{:S(2)}) async-start(bf16[128,64,128]{2,1,0:T(8,128)(2,1)} %bitcast.8), calls=%async_computation.1 | async-start | bytes 4194304 | tf_op jit(solution)/shard_map/all_to_all | solution.py:238

commit v3 on v2

v3 whole, which is shorter than its diff:
```python
import functools
import math

import jax
import jax.numpy as jnp
import ml_dtypes
import numpy as np
from jax import lax
from jax.experimental import pallas as pl
from jax.experimental.pallas import tpu as pltpu
from jax.sharding import PartitionSpec as P

SAMPLES = 1000
BINS = 200
FIRST_BIN = 20
BAND = 256
LAGS = 256
WINDOWS = 256
OWNERS = BINS // 2
OWNER_ROWS = 104
ROWS = 2 * OWNER_ROWS


def cos_sin(freqs, times):
    turns = freqs * times
    turns = turns - SAMPLES * jnp.floor(turns * (1.0 / SAMPLES) + 0.5)
    phase = turns * (2.0 * math.pi / SAMPLES)
    return jnp.cos(phase), jnp.sin(phase)


def dft_rows():
    def ramp(rows, axis):
        return lax.broadcasted_iota(jnp.int32, (rows, SAMPLES), axis).astype(jnp.float32)

    near_cos, near_sin = cos_sin(ramp(8, 0), ramp(8, 1))
    steps = OWNER_ROWS // 8
    place = ramp(2 * 16, 0)
    base = FIRST_BIN + 8.0 * place + jnp.where(place < 16, 0.0, OWNERS - 8.0 * 16)
    base_cos, base_sin = cos_sin(base, ramp(2 * 16, 1))
    real_rows, imag_rows = [], []
    for b in range(2):
        for n in range(steps):
            row = b * 16 + n
            far_cos, far_sin = base_cos[row : row + 1], base_sin[row : row + 1]
            real_rows.append(far_cos * near_cos - far_sin * near_sin)
            imag_rows.append(-far_sin * near_cos - far_cos * near_sin)
    table = jnp.concatenate(real_rows + imag_rows, axis=0)
    place = lax.broadcasted_iota(jnp.int32, (2 * ROWS, 1), 0) % OWNER_ROWS
    return jnp.where(place < OWNERS, table, 0.0).astype(jnp.bfloat16)


def lag_rows():
    shifts = np.arange(LAGS) - LAGS // 2
    bins = np.arange(BINS).reshape(2, OWNERS).T.reshape(-1)
    phase = ((FIRST_BIN + bins)[:, None] * shifts[None, :] % SAMPLES) * (2.0 * math.pi / SAMPLES)
    table = np.stack([np.cos(phase), -np.sin(phase)], axis=1) / (WINDOWS * math.sqrt(BINS))
    table = table.reshape(2 * BINS, LAGS)
    high = table.astype(ml_dtypes.bfloat16)
    low = (table - high.astype(np.float64)).astype(ml_dtypes.bfloat16)
    return np.concatenate([high, low], axis=1)


def dot(left, right, left_dim, right_dim):
    dims = (((left_dim,), (right_dim,)), ((), ()))
    return lax.dot_general(left, right, dims, preferred_element_type=jnp.float32)


def params(mebibytes):
    return pltpu.CompilerParams(vmem_limit_bytes=mebibytes * 1024 * 1024)


def cost(flops, bytes_accessed):
    return pl.CostEstimate(flops=flops, bytes_accessed=bytes_accessed, transcendentals=0)


def bin_of(row):
    return jnp.where(row < OWNER_ROWS, row, row - (OWNER_ROWS - OWNERS))


def near_matrix():
    row = lax.broadcasted_iota(jnp.int32, (ROWS, ROWS), 0)
    column = lax.broadcasted_iota(jnp.int32, (ROWS, ROWS), 1)
    near = jnp.abs(bin_of(row) - bin_of(column)) <= 4
    near = near & (row % OWNER_ROWS < OWNERS) & (column % OWNER_ROWS < OWNERS)
    return jnp.where(near, 1.0, 0.0).astype(jnp.bfloat16)


def whiten_kernel(chunk, records_hbm, out_ref, records_ref, dft_ref, rows_ref, sems):
    windows, _, channels = records_ref.shape
    row_count = rows_ref.shape[1]
    pieces = [(0, begin, chunk) for begin in range(0, channels, chunk)]
    pieces += [(w, 0, channels) for w in range(1, windows)]
    copies = []
    for n, (w, begin, extent) in enumerate(pieces):
        where = (w, slice(None), pl.ds(begin, extent))
        copies.append(pltpu.make_async_copy(records_hbm.at[where], records_ref.at[where], sems.at[n]))
        copies[-1].start()
    near = near_matrix()
    twice = jnp.concatenate([near, near], axis=1)
    place = bin_of(lax.broadcasted_iota(jnp.int32, (ROWS, 1), 0))
    count = jnp.minimum(place + 4, BINS - 1) - jnp.maximum(place - 4, 0) + 1
    weight = 1.0 / count.astype(jnp.float32)
    rest = row_count - OWNER_ROWS * 8
    out_ref[OWNER_ROWS * 8 :, :] = jnp.zeros((rest, channels), jnp.bfloat16)
    dft_ref[...] = dft_rows()
    for copy, (w, begin, extent) in zip(copies, pieces):
        copy.wait()
        spectra = dot(dft_ref[...], records_ref[w, :, begin : begin + extent], 1, 0)
        real_part = spectra[:ROWS]
        imag_part = spectra[ROWS:]
        power = real_part * real_part + imag_part * imag_part
        size = jnp.sqrt(power)
        high = size.astype(jnp.bfloat16)
        low = (size - high.astype(jnp.float32)).astype(jnp.bfloat16)
        smooth = dot(twice, jnp.concatenate([high, low], axis=0), 1, 0) * weight
        level = jnp.sqrt(jnp.sum(power, axis=0, keepdims=True) * (1.0 / BINS) + 1e-06)
        scale = 1.0 / (smooth + 0.25 * level)
        for part, values in enumerate((real_part * scale, imag_part * scale)):
            place = part * windows + w
            for n in range(extent // 128):
                piece = values[:, n * 128 : (n + 1) * 128]
                for b in range(2):
                    rows_ref[begin // 128 + n, pl.ds(b * 4 + place, OWNER_ROWS, stride=8), :] = piece[
                        b * OWNER_ROWS : (b + 1) * OWNER_ROWS
                    ]
        if w == windows - 1:
            for n in range(channels // 128):
                kept = rows_ref[n, : OWNER_ROWS * 8].astype(jnp.bfloat16)
                out_ref[: OWNER_ROWS * 8, n * 128 : (n + 1) * 128] = kept


def whiten(records, devices):
    windows, samples, channels = records.shape
    rows = devices * 8
    chunk = 1024
    return pl.pallas_call(
        functools.partial(whiten_kernel, chunk),
        in_specs=[pl.BlockSpec(memory_space=pltpu.HBM)],
        out_specs=pl.BlockSpec(memory_space=pltpu.VMEM),
        out_shape=jax.ShapeDtypeStruct((rows, channels), jnp.bfloat16),
        scratch_shapes=[
            pltpu.VMEM(records.shape, jnp.bfloat16),
            pltpu.VMEM((2 * ROWS, samples), jnp.bfloat16),
            pltpu.VMEM((channels // 128, rows, 128), jnp.float32),
            pltpu.SemaphoreType.DMA((windows - 1 + channels // chunk,)),
        ],
        compiler_params=params(50),
        cost_estimate=cost(2 * windows * samples * channels * 2 * BINS, records.size * 2 + rows * channels * 2),
        name="whiten",
    )(records)


def stack_kernel(rows_ref, out_ref, plain_ref, turned_ref):
    row_count, channels = rows_ref.shape
    block = 256
    row = lax.broadcasted_iota(jnp.int32, (1, 8, block), 1)
    for begin in range(0, channels, block):
        wide = rows_ref[:, begin : begin + block].astype(jnp.float32).reshape(row_count // 16, 2, 8, block)
        even, odd = wide[:, 0], wide[:, 1]
        halves = (
            jnp.where(row < 4, even, pltpu.roll(odd, 4, 1)),
            jnp.where(row < 4, pltpu.roll(even, 4, 1), odd),
        )
        for b, half in enumerate(halves):
            turned = jnp.where(row // 2 % 2 == 0, pltpu.roll(half, 6, 1), -pltpu.roll(half, 2, 1))
            for ref, value in ((plain_ref, half), (turned_ref, turned)):
                ref[b, :, begin : begin + block] = value.reshape(row_count // 2, block).astype(jnp.bfloat16)
    row = lax.broadcasted_iota(jnp.int32, (block, block), 0)
    column = lax.broadcasted_iota(jnp.int32, (block, block), 1)
    flip = jnp.where(row + column == block - 1, 1.0, 0.0).astype(jnp.bfloat16)
    lane = lax.broadcasted_iota(jnp.int32, (16, 128), 1)
    for c in range(channels // block):
        begin = c * block
        sources = [ref[b, :, begin : begin + block] for b in range(2) for ref in (plain_ref, turned_ref)]
        flipped = dot(flip, jnp.concatenate(sources, axis=0), 1, 1).astype(jnp.bfloat16)
        count = row_count // 2
        for b in range(2):
            sides = [flipped[:, (2 * b + n) * count : (2 * b + n + 1) * count] for n in range(2)]
            left = jnp.concatenate(sides, axis=0)
            extent = min(512, channels - begin)
            products = dot(left, plain_ref[b, :, begin : begin + extent], 1, 0)
            if extent < 512:
                products = jnp.concatenate([products, jnp.zeros((512, 512 - extent), jnp.float32)], axis=1)
            for p in range(2):
                item = (b * 2 + p) * 16
                for i in range(8):
                    u, j = i // 4, i % 4
                    r = p * 256 + i * 32
                    part = products[r : r + 32, 128 * (1 - u) : 128 * (1 - u) + 384]
                    second = pltpu.roll(part[:16], (321 + 32 * j) % 384, 1, stride=1, stride_axis=0)
                    first = pltpu.roll(part[16:], (273 + 32 * j) % 384, 1, stride=1, stride_axis=0)
                    where = c * 8 + 7 - i
                    for q in range(2):
                        now = slice(q * 128, (q + 1) * 128)
                        then = slice((q + 1) * 128, (q + 2) * 128)
                        low = jnp.where(lane < 64, first[:, now], second[:, now])
                        high = jnp.where(lane < 64, second[:, then], first[:, now])
                        out_ref[where, 2 * q, item : item + 16, :] = low.astype(jnp.bfloat16)
                        out_ref[where, 2 * q + 1, item : item + 16, :] = high.astype(jnp.bfloat16)


def stack(rows, chan_size, win_size):
    row_count, channels = rows.shape
    return pl.pallas_call(
        stack_kernel,
        out_shape=jax.ShapeDtypeStruct((chan_size, win_size, 64, 128), jnp.bfloat16),
        in_specs=[pl.BlockSpec(memory_space=pltpu.VMEM)],
        out_specs=pl.BlockSpec(memory_space=pltpu.VMEM),
        scratch_shapes=[pltpu.VMEM((2, row_count // 2, channels), jnp.bfloat16)] * 2,
        compiler_params=params(24),
        cost_estimate=cost(4 * 2 * 1024 * 512 * 512, 4 * 1024 * 1024),
        name="stack",
    )(rows)


def lag_kernel(parts, swap_ref, table_ref, stacks_ref, out_hbm, wide_ref, out_ref, sems):
    items = table_ref.shape[0]
    each = 16 // parts
    wide_ref[...] = stacks_ref[...].astype(jnp.float32)
    swap = swap_ref[0]
    copies = []
    for part in range(parts):
        sides = []
        for n in range(each):
            place = 15 - (part * each + n)
            sides.append(wide_ref[pl.ds(place, items, stride=16), :].astype(jnp.bfloat16))
        both = dot(jnp.concatenate(sides, axis=1), table_ref[...], 0, 0)
        lags = both[:, :LAGS] + both[:, LAGS:]
        for n in range(each):
            for h in range(2):
                r = n * 128 + h * 64
                out_ref[(h + swap) % 2, part * each + n] = lags[r : r + 64]
        where = (slice(None), pl.ds(part * each, each))
        copies.append(pltpu.make_async_copy(out_ref.at[where], out_hbm.at[where], sems.at[part]))
        copies[-1].start()
    for copy in copies:
        copy.wait()


def lag_transform(stacks, swap):
    parts = 4
    table = jnp.asarray(lag_rows())
    rows = 2 * BINS * 16
    shape = (2, 16, 64, LAGS)
    out = pl.pallas_call(
        functools.partial(lag_kernel, parts),
        grid=(1,),
        in_specs=[
            pl.BlockSpec(memory_space=pltpu.SMEM),
            pl.BlockSpec(table.shape, lambda i: (0, 0)),
            pl.BlockSpec((rows, 128), lambda i: (0, 0)),
        ],
        out_specs=pl.BlockSpec(memory_space=pltpu.HBM),
        out_shape=jax.ShapeDtypeStruct(shape, jnp.float32),
        scratch_shapes=[
            pltpu.VMEM((rows, 128), jnp.float32),
            pltpu.VMEM(shape, jnp.float32),
            pltpu.SemaphoreType.DMA((parts,)),
        ],
        compiler_params=params(24),
        cost_estimate=cost(4 * 2 * BINS * 2048 * 256, 4 * 1024 * 1024),
        name="lag_transform",
    )(swap, table, stacks)
    return out.reshape(32, 64, LAGS)


def per_device(chan_size, win_size, records):
    devices = chan_size * win_size
    axes = ("chan", "win")
    channels = records.shape[2]
    swap = jnp.full((1,), lax.axis_index("win") % 2, jnp.int32)
    rows = whiten(records, devices).reshape(devices, 8, channels)
    rows, swap = lax.optimization_barrier((rows, swap))
    rows = lax.all_to_all(rows, axes, split_axis=0, concat_axis=0, tiled=True)
    stacks = stack(rows.reshape(devices * 8, channels), chan_size, win_size)
    stacks = stacks.reshape(devices, 64, 128)
    stacks = lax.all_to_all(stacks, axes, split_axis=0, concat_axis=0, tiled=True)
    return lag_transform(stacks.reshape(devices * 64, 128), swap)


def solution(mesh):
    in_specs = (P(("chan", "win"), None, None),)
    out_specs = P("chan", "win", None)
    body = functools.partial(per_device, mesh.shape["chan"], mesh.shape["win"])
    return jax.shard_map(body, mesh=mesh, in_specs=in_specs, out_specs=out_specs, check_vma=False)
```

time: 95.8 us -> 88.4 us (0.923)
  blocking collectives: 41.4 us -> 76 us
  waiting for transfers between devices: 30.2 us -> 0 us
  starting transfers between devices: 4.89 us -> 0 us
  Pallas kernels: 16.6 us -> 12.2 us
  local copies, waits for them, and re-layouts: 2.47 us -> 0.01 us
    all_to_all x0 -> x1, blocking collectives: none -> 34.6 us  [per_device(): lax.all_to_all(stacks, axes, split_axis=0, concat_axis=0, tiled=True)]
    all_to_all x1 -> x0, waiting for transfers between devices: 30.2 us -> none  [per_device(): lax.all_to_all(stacks, axes, split_axis=0, concat_axis=0, tiled=True)]
    all_to_all x1 -> x0, starting transfers between devices: 4.89 us -> none  [per_device(): lax.all_to_all(stacks, axes, split_axis=0, concat_axis=0, tiled=True)]
    unnamed x6 -> x2, local copies, waits for them, and re-layouts: 2.47 us -> 0.01 us
    pallas_call x2, Pallas kernels: 10.7 us -> 8.36 us  [the longest x1 4.99 us: whiten(): pl.pallas_call(functools.partial(whiten_kernel, chunk), in_specs=[pl.Bloc...]
    pallas_call x1, Pallas kernels: 5.92 us -> 3.88 us  [stack(): pl.pallas_call(stack_kernel, out_shape=jax.ShapeDtypeStruct((chan_size, w...]
  transfers between devices with their start and end apart: 1 -> 0, of which waited for: 1 -> 0; matrix products, arithmetic and copies ran while one was open for 0% -> 0% of each run, Pallas kernels for 0% -> 0%
where the time goes in v3:
time: 88.4 us; the launch traced here: 88.2 us
  blocking collectives  76 us (86%)
  Pallas kernels  12.2 us (14%)
    all_to_all x1, blocking collectives, per_device(): rows = lax.all_to_all(rows, axes, split_axis=0, concat_axis=0, tiled=True)  41.3 us
    all_to_all x1, blocking collectives, per_device(): lax.all_to_all(stacks, axes, split_axis=0, concat_axis=0, tiled=True)  34.6 us
    pallas_call x1, Pallas kernels, whiten(): pl.pallas_call(functools.partial(whiten_kernel, chunk), in_specs=[pl.Bloc...  4.99 us
    pallas_call x1, Pallas kernels, stack(): pl.pallas_call(stack_kernel, out_shape=jax.ShapeDtypeStruct((chan_size, w...  3.88 us
    pallas_call x1, Pallas kernels, lag_transform(): pl.pallas_call(functools.partial(lag_kernel, parts), grid=(1,), in_specs=...  3.37 us

profile of v3, /device:TPU:1, one launch (start us, length us, event | category | flops | bytes accessed | tf_op | source)
XLA Modules:
  0.0 88.2 jit_solution(17936407485557685008)
XLA Ops:
  0.0 5.0 %whiten.1 = bf16[1024,1024]{1,0:T(8,128)(2,1)S(1)} custom-call(bf16[2,1000,1024]{2,1,0:T(8,128)(2,1)} %records_hbm.1), custom_call_target="tpu_custom_call" | custom-call | flops 1638400000 | bytes 6193152 | tf_op jit(solution)/shard_map/whiten/pallas_call | solution.py:136
  5.0 41.3 %all_to_all.10 = bf16[128,8,1024]{2,1,0:T(8,128)(2,1)S(1)} all-to-all(bf16[128,8,1024]{2,1,0:T(8,128)(2,1)S(1)} %bitcast.6), channel_id=1, replica_groups=mesh['chan'=32,'win'=4] {'chan','win'}, dimensions={0} | all-to-all | bytes 4194304 | tf_op jit(solution)/shard_map/all_to_all | solution.py:274
  46.3 3.9 %stack.1 = bf16[32,4,64,128]{3,2,1,0:T(8,128)(2,1)S(1)} custom-call(bf16[1024,1024]{1,0:T(8,128)(2,1)S(1)} %bitcast.8), custom_call_target="tpu_custom_call" | custom-call | flops 2147483648 | bytes 4194304 | tf_op jit(solution)/shard_map/stack/pallas_call | solution.py:204
  50.2 0.0 copy-start
  50.2 34.6 %all_to_all.11 = bf16[128,64,128]{2,1,0:T(8,128)(2,1)S(1)} all-to-all(bf16[128,64,128]{2,1,0:T(8,128)(2,1)S(1)} %bitcast.9), channel_id=1, replica_groups=mesh['chan'=32,'win'=4] {'chan','win'}, dimensions={0} | all-to-all | bytes 4194304 | tf_op jit(solution)/shard_map/all_to_all | solution.py:277
  84.9 0.0 copy-done
  84.9 3.4 %lag_transform.1 = f32[2,16,64,256]{3,2,1,0:T(8,128)} custom-call(s32[1]{0:T(128)} %bitcast.1.swap_ref, bf16[400,512]{1,0:T(8,128)(2,1)S(1)} %copy-done, bf16[8192,128]{1,0:T(8,128)(2,1)S(1)} %bitcast.7), custom_call_target="tpu_custom_call" | custom-call | flops 838860800 | bytes 4194304 | tf_op jit(solution)/shard_map/lag_transform/pallas_call | solution.py:245
Async XLA Ops:
  50.2 34.6 %copy-start = (bf16[400,512]{1,0:T(8,128)(2,1)S(1)}, bf16[400,512]{1,0:T(8,128)(2,1)}, u32[]{:S(2)}) copy-start(bf16[400,512]{1,0:T(8,128)(2,1)} %constant.19.clone.table_ref) | copy-start | bytes 1228804

commit v4 on v3

v4 whole, which is shorter than its diff:
```python
import functools
import math

import jax
import jax.numpy as jnp
import ml_dtypes
import numpy as np
from jax import lax
from jax.experimental import pallas as pl
from jax.experimental.pallas import tpu as pltpu
from jax.sharding import PartitionSpec as P

SAMPLES = 1000
BINS = 200
FIRST_BIN = 20
BAND = 256
LAGS = 256
WINDOWS = 256
GROUP = 8
REACH = 384


def cos_sin(freqs, times):
    turns = freqs * times
    turns = turns - SAMPLES * jnp.floor(turns * (1.0 / SAMPLES) + 0.5)
    phase = turns * (2.0 * math.pi / SAMPLES)
    return jnp.cos(phase), jnp.sin(phase)


def dft_rows():
    def ramp(rows, axis):
        return lax.broadcasted_iota(jnp.int32, (rows, SAMPLES), axis).astype(jnp.float32)

    near_cos, near_sin = cos_sin(ramp(8, 0), ramp(8, 1))
    base_cos, base_sin = cos_sin(FIRST_BIN + 8.0 * ramp(32, 0), ramp(32, 1))
    real_rows, imag_rows = [], []
    for n in range(BINS // 8):
        far_cos, far_sin = base_cos[n : n + 1], base_sin[n : n + 1]
        real_rows.append(far_cos * near_cos - far_sin * near_sin)
        imag_rows.append(-far_sin * near_cos - far_cos * near_sin)
    return jnp.concatenate(real_rows + imag_rows, axis=0).astype(jnp.bfloat16)


def lag_rows(devices):
    owner = np.arange(devices)
    third = devices + owner // 2
    bins = np.stack([owner, owner, third], axis=1).reshape(-1)
    part = np.stack([0 * owner, 0 * owner + 1, owner % 2], axis=1).reshape(-1)
    last = np.arange(BINS - GROUP, BINS)
    bins = np.concatenate([bins, np.repeat(last, 2)])
    part = np.concatenate([part, np.tile([0, 1], GROUP)])
    shifts = np.arange(LAGS) - LAGS // 2
    phase = ((FIRST_BIN + bins)[:, None] * shifts[None, :] % SAMPLES) * (2.0 * math.pi / SAMPLES)
    table = np.where(part[:, None] == 0, np.cos(phase), -np.sin(phase)) / (WINDOWS * math.sqrt(BINS))
    high = table.astype(ml_dtypes.bfloat16)
    low = (table - high.astype(np.float64)).astype(ml_dtypes.bfloat16)
    return np.concatenate([high, low], axis=1)


def dot(left, right, left_dim, right_dim):
    dims = (((left_dim,), (right_dim,)), ((), ()))
    return lax.dot_general(left, right, dims, preferred_element_type=jnp.float32)


def params(mebibytes):
    return pltpu.CompilerParams(vmem_limit_bytes=mebibytes * 1024 * 1024)


def cost(flops, bytes_accessed):
    return pl.CostEstimate(flops=flops, bytes_accessed=bytes_accessed, transcendentals=0)


def whiten_kernel(devices, records_hbm, out_ref, records_ref, dft_ref, rows_ref, sems):
    windows, _, channels = records_ref.shape
    copies = []
    for w in range(windows):
        copies.append(pltpu.make_async_copy(records_hbm.at[w], records_ref.at[w], sems.at[w]))
        copies[-1].start()
    row = lax.broadcasted_iota(jnp.int32, (BINS, BINS), 0)
    column = lax.broadcasted_iota(jnp.int32, (BINS, BINS), 1)
    near = jnp.where(jnp.abs(row - column) <= 4, 1.0, 0.0).astype(jnp.bfloat16)
    place = lax.broadcasted_iota(jnp.int32, (BINS, 1), 0)
    count = jnp.minimum(place + 4, BINS - 1) - jnp.maximum(place - 4, 0) + 1
    weight = 1.0 / count.astype(jnp.float32)
    for part in range(2):
        for half in range(2):
            rows_ref[4 * half + 3, pl.ds(6 + part, devices, stride=8), :] = jnp.zeros((devices, 128), jnp.float32)
    dft_ref[...] = dft_rows()
    for w in range(windows):
        copies[w].wait()
        spectra = dot(dft_ref[...], records_ref[w], 1, 0)
        real_part = spectra[:BINS]
        imag_part = spectra[BINS:]
        power = real_part * real_part + imag_part * imag_part
        size = jnp.sqrt(power)
        high = size.astype(jnp.bfloat16)
        low = (size - high.astype(jnp.float32)).astype(jnp.bfloat16)
        smooth = (dot(near, high, 1, 0) + dot(near, low, 1, 0)) * weight
        level = jnp.sqrt(jnp.sum(power, axis=0, keepdims=True) * (1.0 / BINS) + 1e-06)
        scale = 1.0 / (smooth + 0.25 * level)
        for part, values in enumerate((real_part * scale, imag_part * scale)):
            for n in range(channels // 128):
                piece = values[:, n * 128 : (n + 1) * 128]
                rows_ref[n, pl.ds(part * 2 + w, devices, stride=8), :] = piece[:devices]
                rows_ref[n, pl.ds(w * 8 + 4 + part, devices // 2, stride=16), :] = piece[devices : BINS - GROUP]
            last = values[BINS - GROUP :]
            last = jnp.concatenate([last, jnp.zeros((GROUP, REACH), jnp.float32)], axis=1)
            for g in range(devices // GROUP):
                begin = g * (channels * GROUP // devices)
                reach = last[:, begin : begin + REACH]
                for n in range(REACH // 128):
                    where = pl.ds(g * GROUP * 8 + 6 + part, GROUP, stride=8)
                    rows_ref[4 * w + n, where, :] = reach[:, n * 128 : (n + 1) * 128]
    for n in range(channels // 128):
        out_ref[:, n * 128 : (n + 1) * 128] = rows_ref[n].astype(jnp.bfloat16)


def whiten(records, devices):
    windows, samples, channels = records.shape
    rows = devices * 8
    return pl.pallas_call(
        functools.partial(whiten_kernel, devices),
        in_specs=[pl.BlockSpec(memory_space=pltpu.HBM)],
        out_specs=pl.BlockSpec(memory_space=pltpu.VMEM),
        out_shape=jax.ShapeDtypeStruct((rows, channels), jnp.bfloat16),
        scratch_shapes=[
            pltpu.VMEM(records.shape, jnp.bfloat16),
            pltpu.VMEM((2 * BINS, samples), jnp.bfloat16),
            pltpu.VMEM((channels // 128, rows, 128), jnp.float32),
            pltpu.SemaphoreType.DMA((windows,)),
        ],
        compiler_params=params(50),
        cost_estimate=cost(2 * windows * samples * channels * 2 * BINS, records.size * 2 + rows * channels * 2),
        name="whiten",
    )(records)


def split_rows(even, odd, gap):
    row = lax.broadcasted_iota(jnp.int32, (1, 8, even.shape[2]), 1)
    first = row // gap % 2 == 0
    return jnp.where(first, even, pltpu.roll(odd, gap, 1)), jnp.where(first, pltpu.roll(even, 8 - gap, 1), odd)


def compact_kernel(rows_ref, own_ref, shared_ref, last_ref):
    row_count, channels = rows_ref.shape
    block = 256

    def halves(value):
        value = value.reshape(value.shape[0] // 2, 2, 8, block)
        return value[:, 0], value[:, 1]

    for begin in range(0, channels, block):
        now = slice(begin, begin + block)
        wide = rows_ref[:, now].astype(jnp.float32).reshape(row_count // 8, 8, block)
        own, rest = split_rows(*halves(wide), 4)
        shared, last = split_rows(*halves(rest), 2)
        for ref, value, gap in ((own_ref, own, 2), (shared_ref, shared, 1), (last_ref, last, 1)):
            for part, piece in enumerate(split_rows(*halves(value), gap)):
                count = ref.shape[0] // 2
                ref[part * count : (part + 1) * count, now] = piece.reshape(count, block).astype(jnp.bfloat16)


def compact(rows):
    row_count, channels = rows.shape
    shapes = [row_count // 2, row_count // 4, row_count // 4]
    return pl.pallas_call(
        compact_kernel,
        out_shape=[jax.ShapeDtypeStruct((n, channels), jnp.bfloat16) for n in shapes],
        in_specs=[pl.BlockSpec(memory_space=pltpu.VMEM)],
        out_specs=[pl.BlockSpec(memory_space=pltpu.VMEM)] * 3,
        compiler_params=params(16),
        cost_estimate=cost(0, 4 * 1024 * 1024),
        name="compact",
    )(rows)


def flip_matrix(count, width):
    row = lax.broadcasted_iota(jnp.int32, (count, width), 0)
    column = lax.broadcasted_iota(jnp.int32, (count, width), 1)
    return jnp.where(row + column == count - 1, 1.0, 0.0).astype(jnp.bfloat16)


def turned(left, width):
    pieces = []
    for begin in range(0, left.shape[1], 2 * width):
        pieces += [left[:, begin + width : begin + 2 * width], -left[:, begin : begin + width]]
    return jnp.concatenate(pieces, axis=1)


def skew_store(part, shift, lane, store):
    second = pltpu.roll(part[:16], (shift + 64) % REACH, 1, stride=1, stride_axis=0)
    first = pltpu.roll(part[16:], (shift + 16) % REACH, 1, stride=1, stride_axis=0)
    for q in range(BAND // 128):
        now = slice(q * 128, (q + 1) * 128)
        then = slice((q + 1) * 128, (q + 2) * 128)
        store(2 * q, jnp.where(lane < 64, first[:, now], second[:, now]).astype(jnp.bfloat16))
        store(2 * q + 1, jnp.where(lane < 64, second[:, then], first[:, now]).astype(jnp.bfloat16))


def store_items(products, c, item, out_ref, lane):
    for i in range(8):
        begin = 128 * (1 - i // 4)
        part = products[i * 32 : (i + 1) * 32, begin : begin + REACH]

        def store(j, value, i=i):
            out_ref[(c * 8 + 7 - i) * 4 + j, item * 16 : (item + 1) * 16, :] = value

        skew_store(part, 257 + 32 * (i % 4), lane, store)


def band_products(left, right_ref, begin, width):
    extent = min(width, right_ref.shape[1] - begin)
    products = dot(left, right_ref[:, begin : begin + extent], 1, 0)
    if extent < width:
        products = jnp.concatenate([products, jnp.zeros((left.shape[0], width - extent), jnp.float32)], axis=1)
    return products


def stack_kernel(info_ref, own_ref, last_ref, out_ref, mine_ref, pair_ref, rest_ref):
    row_count, channels = own_ref.shape
    block = 256
    lane = lax.broadcasted_iota(jnp.int32, (16, 128), 1)
    wide = jnp.concatenate([last_ref[:, :REACH], last_ref[:, 512 : 512 + REACH]], axis=0)
    left = dot(flip_matrix(64, 128), wide[:, :128], 1, 1).astype(jnp.bfloat16)
    left = jnp.concatenate([left, turned(left, row_count // 4)], axis=0)
    products = dot(left, wide, 1, 0)
    for p in range(2):
        for i in range(2):

            def store(j, value, p=p, i=i):
                rest_ref[jnp.where(info_ref[1] == 1 - i, 0, 1), j, p * 16 : (p + 1) * 16, :] = value

            r = p * 64 + i * 32
            skew_store(products[r : r + 32], REACH - 63 + 32 * i, lane, store)
    mine_ref[...] = rest_ref[0]
    pair_ref[...] = rest_ref[1]
    flip = flip_matrix(block, block)
    for c in range(channels // block):
        left = dot(flip, own_ref[:, c * block : (c + 1) * block], 1, 1).astype(jnp.bfloat16)
        left = jnp.concatenate([left, turned(left, row_count // 2)], axis=0)
        products = band_products(left, own_ref, c * block, 2 * block)
        for p in range(2):
            store_items(products[p * block : (p + 1) * block], c, p, out_ref, lane)


def stack(info, own, last, devices):
    shapes = [(devices, 32, 128), (4, 32, 128), (4, 32, 128)]
    return pl.pallas_call(
        stack_kernel,
        out_shape=[jax.ShapeDtypeStruct(shape, jnp.bfloat16) for shape in shapes],
        in_specs=[pl.BlockSpec(memory_space=pltpu.SMEM)] + [pl.BlockSpec(memory_space=pltpu.VMEM)] * 2,
        out_specs=[pl.BlockSpec(memory_space=pltpu.VMEM)] * 3,
        scratch_shapes=[pltpu.VMEM((2, 4, 32, 128), jnp.bfloat16)],
        compiler_params=params(16),
        cost_estimate=cost(4 * 1024 * 512 * 512, 4 * 1024 * 1024),
        name="stack",
    )(info, own, last)


def shared_kernel(info_ref, own_ref, other_ref, items_ref, out_hbm, both_ref, item_ref, sems):
    row_count, channels = own_ref.shape
    block = 256
    copies = [pltpu.make_async_copy(items_ref, out_hbm.at[:, pl.ds(0, 32)], sems.at[0])]
    copies[0].start()
    lane = lax.broadcasted_iota(jnp.int32, (16, 128), 1)
    both_ref[:row_count] = own_ref[...]
    both_ref[row_count:] = other_ref[...]
    core = info_ref[0]
    flip = flip_matrix(block, block)
    for c in range(channels // block):
        left = dot(flip, both_ref[:, c * block : (c + 1) * block], 1, 1).astype(jnp.bfloat16)
        left = jnp.where(core == 0, left, turned(left, row_count // 2))
        products = band_products(left, both_ref, c * block, 2 * block)
        store_items(products, c, 0, item_ref, lane)
        where = pl.ds(c * 32, 32)
        copies.append(
            pltpu.make_async_copy(item_ref.at[where], out_hbm.at[where, pl.ds(32, 16)], sems.at[c + 1])
        )
        copies[-1].start()
    for copy in copies:
        copy.wait()


def stack_shared(info, own, other, items, devices):
    row_count, channels = own.shape
    return pl.pallas_call(
        shared_kernel,
        out_shape=jax.ShapeDtypeStruct((devices, 48, 128), jnp.bfloat16),
        in_specs=[pl.BlockSpec(memory_space=pltpu.SMEM)] + [pl.BlockSpec(memory_space=pltpu.VMEM)] * 3,
        out_specs=pl.BlockSpec(memory_space=pltpu.HBM),
        scratch_shapes=[
            pltpu.VMEM((2 * row_count, channels), jnp.bfloat16),
            pltpu.VMEM((devices, 16, 128), jnp.bfloat16),
            pltpu.SemaphoreType.DMA((1 + channels // 256,)),
        ],
        compiler_params=params(16),
        cost_estimate=cost(2 * 1024 * 512 * 512, 4 * 1024 * 1024),
        name="stack_shared",
    )(info, own, other, items)


def lag_kernel(parts, info_ref, table_ref, stacks_ref, mine_ref, pair_ref, out_hbm, wide_ref, out_ref, sems):
    items = table_ref.shape[0]
    each = 16 // parts
    split = stacks_ref.shape[0]
    wide_ref[:split] = stacks_ref[...].astype(jnp.float32)
    mine, win = info_ref[1], info_ref[2]
    for half, ref in ((mine, mine_ref), (1 - mine, pair_ref)):
        for n in range(4):
            begin = pl.multiple_of(split + (half * 4 + n) * 32, 32)
            wide_ref[pl.ds(begin, 32), :] = ref[n, win].astype(jnp.float32)
    swap = info_ref[0]
    copies = []
    for part in range(parts):
        sides = []
        for n in range(each):
            place = 15 - (part * each + n)
            sides.append(wide_ref[pl.ds(place, items, stride=16), :].astype(jnp.bfloat16))
        both = dot(jnp.concatenate(sides, axis=1), table_ref[...], 0, 0)
        lags = both[:, :LAGS] + both[:, LAGS:]
        for n in range(each):
            for h in range(2):
                r = n * 128 + h * 64
                out_ref[(h + swap) % 2, part * each + n] = lags[r : r + 64]
        where = (slice(None), pl.ds(part * each, each))
        copies.append(pltpu.make_async_copy(out_ref.at[where], out_hbm.at[where], sems.at[part]))
        copies[-1].start()
    for copy in copies:
        copy.wait()


def lag_transform(info, stacks, mine, pair, devices):
    parts = 8
    table = jnp.asarray(lag_rows(devices))
    shape = (2, 16, 64, LAGS)
    out = pl.pallas_call(
        functools.partial(lag_kernel, parts),
        in_specs=[pl.BlockSpec(memory_space=pltpu.SMEM)] + [pl.BlockSpec(memory_space=pltpu.VMEM)] * 4,
        out_specs=pl.BlockSpec(memory_space=pltpu.HBM),
        out_shape=jax.ShapeDtypeStruct(shape, jnp.float32),
        scratch_shapes=[
            pltpu.VMEM((2 * BINS * 16, 128), jnp.float32),
            pltpu.VMEM(shape, jnp.float32),
            pltpu.SemaphoreType.DMA((parts,)),
        ],
        compiler_params=params(24),
        cost_estimate=cost(4 * 2 * BINS * 2048 * 256, 4 * 1024 * 1024),
        name="lag_transform",
    )(info, table, stacks, mine, pair)
    return out.reshape(32, 64, LAGS)


def per_device(chan_size, win_size, records):
    devices = chan_size * win_size
    axes = ("chan", "win")
    channels = records.shape[2]

    def exchange(array):
        return lax.all_to_all(array, axes, split_axis=0, concat_axis=0, tiled=True)

    win = lax.axis_index("win")
    info = jnp.stack([win % 2, lax.axis_index("chan") % 2, win]).astype(jnp.int32)
    rows = whiten(records, devices).reshape(devices, 8, channels)
    rows, info = lax.optimization_barrier((rows, info))
    own, shared, last = compact(exchange(rows).reshape(devices * 8, channels))
    other = lax.ppermute(shared, "win", [(w, w ^ 1) for w in range(win_size)])
    items, mine, pair = stack(info, own, last, devices)
    pair = lax.ppermute(pair, "chan", [(c, c ^ 1) for c in range(chan_size)])
    mine = lax.all_gather(mine, "win")
    pair = lax.all_gather(pair, "win")
    stacks = exchange(stack_shared(info, shared, other, items, devices))
    return lag_transform(info, stacks.reshape(devices * 48, 128), mine, pair, devices)


def solution(mesh):
    in_specs = (P(("chan", "win"), None, None),)
    out_specs = P("chan", "win", None)
    body = functools.partial(per_device, mesh.shape["chan"], mesh.shape["win"])
    return jax.shard_map(body, mesh=mesh, in_specs=in_specs, out_specs=out_specs, check_vma=False)
```

time: 88.4 us -> 87.5 us (0.990)
  the two profiles are of different devices: /device:TPU:1 before, /device:TPU:21 now
where the time goes in v4:
time: 87.5 us; the launch traced here: 86.8 us
  blocking collectives  60.9 us (70%)
  Pallas kernels  15.6 us (18%)
  starting transfers between devices  10.2 us (12%)
    all_to_all x1, blocking collectives, exchange(): return lax.all_to_all(array, axes, split_axis=0, concat_axis=0, tiled=True)  36.9 us
    all_gather x1, blocking collectives, per_device(): mine = lax.all_gather(mine, 'win')  18.6 us
    all_to_all x1, starting transfers between devices, exchange(): return lax.all_to_all(array, axes, split_axis=0, concat_axis=0, tiled=True)  7.72 us
    pallas_call x1, Pallas kernels, whiten(): pl.pallas_call(functools.partial(whiten_kernel, devices), in_specs=[pl.Bl...  5.66 us
    all_gather x1, blocking collectives, per_device(): pair = lax.all_gather(pair, 'win')  5.41 us
    pallas_call x1, Pallas kernels, lag_transform(): pl.pallas_call(functools.partial(lag_kernel, parts), in_specs=[pl.BlockSp...  3.7 us
    pallas_call x1, Pallas kernels, stack(): pl.pallas_call(stack_kernel, out_shape=[jax.ShapeDtypeStruct(shape, jnp.b...  2.59 us
    pallas_call x1, Pallas kernels, stack_shared(): pl.pallas_call(shared_kernel, out_shape=jax.ShapeDtypeStruct((devices, 48...  2.59 us
  transfers between devices with their start and end apart: 3, of which 0 were waited for; matrix products, arithmetic and copies ran while one was open for 0% of the time, Pallas kernels for 3%

profile of v4, /device:TPU:21, one launch (start us, length us, event | category | flops | bytes accessed | tf_op | source)
XLA Modules:
  0.0 86.8 jit_solution(8129022712845195369)
XLA Ops:
  0.0 5.7 %whiten.1 = bf16[1024,1024]{1,0:T(8,128)(2,1)S(1)} custom-call(bf16[2,1000,1024]{2,1,0:T(8,128)(2,1)} %records_hbm.1), custom_call_target="tpu_custom_call" | custom-call | flops 1638400000 | bytes 6193152 | tf_op jit(solution)/shard_map/whiten/pallas_call | solution.py:121
  5.7 0.1 pad_add_fusion.info_ref
  5.8 36.9 %all_to_all.10 = bf16[128,8,1024]{2,1,0:T(8,128)(2,1)S(1)} all-to-all(bf16[128,8,1024]{2,1,0:T(8,128)(2,1)S(1)} %bitcast.9), channel_id=1, replica_groups=mesh['chan'=32,'win'=4] {'chan','win'}, dimensions={0} | all-to-all | bytes 4194304 | tf_op jit(solution)/shard_map/all_to_all | solution.py:359
  42.6 1.1 %compact.1 = (bf16[512,1024]{1,0:T(8,128)(2,1)S(1)}, bf16[256,1024]{1,0:T(8,128)(2,1)S(1)}, bf16[256,1024]{1,0:T(8,128)(2,1)S(1)}) custom-call(bf16[1024,1024]{1,0:T(8,128)(2,1)S(1)} %bitcast.10), custom_call_target="tpu_custom_call" | custom-call | bytes 4194304 | tf_op jit(solution)/shard_map/compact/pallas_call | solution.py:166
  43.7 1.0 %collective-permute-start = (bf16[256,1024]{1,0:T(8,128)(2,1)S(1)}, bf16[256,1024]{1,0:T(8,128)(2,1)S(1)}, u32[]{:S(2)}, u32[]{:S(2)}) collective-permute-start(bf16[256,1024]{1,0:T(8,128)(2,1)S(1)} %get-tuple-element.15.own_ref), channel_id=1, source_target_pairs={{0,1},{1,0},{2,3},{3,2},{4,5},{5,4},{6,7},{7,6},{8,9},{9,8},{10,11... | collective-permute-start | bytes 1572872 | tf_op jit(solution)/shard_map/ppermute | solution.py:366
  44.7 2.6 %stack.17 = (bf16[128,32,128]{2,1,0:T(8,128)(2,1)S(1)}, bf16[4,32,128]{2,1,0:T(8,128)(2,1)S(1)}, bf16[4,32,128]{2,1,0:T(8,128)(2,1)S(1)}) custom-call(s32[3]{0:T(128)S(1)} %pad_add_fusion.info_ref, bf16[512,1024]{1,0:T(8,128)(2,1)S(1)} %get-tuple-element.16.own_ref, bf16[256,1024]{1,0:T(8,128)(2,1)S(1)} %get-tuple-element.17.last_ref), custom_call_target="tpu_custom_call" | custom-call | flops 1073741824 | bytes 4194304 | tf_op jit(solution)/shard_map/stack/pallas_call | solution.py:248
  47.3 0.0 collective-permute-done.other_ref
  47.3 2.6 %stack_shared.1 = bf16[128,48,128]{2,1,0:T(8,128)(2,1)} custom-call(s32[3]{0:T(128)S(1)} %pad_add_fusion.info_ref, bf16[256,1024]{1,0:T(8,128)(2,1)S(1)} %get-tuple-element.15.own_ref, bf16[256,1024]{1,0:T(8,128)(2,1)S(1)} %collective-permute-done.other_ref, bf16[128,32,128]{2,1,0:T(8,128)(2,1)S(1)} %get-tuple-element.18.items_ref), custom_call_target="tpu_custom_call" | custom-call | flops 536870912 | bytes 4194304 | tf_op jit(solution)/shard_map/stack_shared/pallas_call | solution.py:286
  49.9 0.0 copy-start
  49.9 7.7 %all-to-all-start.1 = ((bf16[128,48,128]{2,1,0:T(8,128)(2,1)}), bf16[128,48,128]{2,1,0:T(8,128)(2,1)S(1)}, u32[]{:S(2)}, u32[]{:S(2)}) async-start(bf16[128,48,128]{2,1,0:T(8,128)(2,1)} %stack_shared.1), calls=%async_computation.1 | async-start | bytes 3145728 | tf_op jit(solution)/shard_map/all_to_all | solution.py:359
  57.6 1.5 %collective-permute-start.1 = (bf16[4,32,128]{2,1,0:T(8,128)(2,1)S(1)}, bf16[4,32,128]{2,1,0:T(8,128)(2,1)S(1)}, u32[]{:S(2)}, u32[]{:S(2)}) collective-permute-start(bf16[4,32,128]{2,1,0:T(8,128)(2,1)S(1)} %get-tuple-element.20), channel_id=1, source_target_pairs={{0,4},{4,0},{8,12},{12,8},{16,20},{20,16},{24,28},{28,24},{32,36},... | collective-permute-start | bytes 98312 | tf_op jit(solution)/shard_map/ppermute | solution.py:368
  59.1 18.6 %all-gather = bf16[16,32,128]{2,1,0:T(8,128)(2,1)S(1)} all-gather(bf16[4,32,128]{2,1,0:T(8,128)(2,1)S(1)} %get-tuple-element.19), channel_id=2, replica_groups=mesh['chan'=32,'win'=4] {'win'}, dimensions={0}, use_global_device_ids=true | all-gather | bytes 163840 | tf_op jit(solution)/shard_map/all_gather | solution.py:369
  77.7 0.0 collective-permute-done.1
  77.7 5.4 %all-gather.1 = bf16[16,32,128]{2,1,0:T(8,128)(2,1)S(1)} all-gather(bf16[4,32,128]{2,1,0:T(8,128)(2,1)S(1)} %collective-permute-done.1), channel_id=3, replica_groups=mesh['chan'=32,'win'=4] {'win'}, dimensions={0}, use_global_device_ids=true | all-gather | bytes 163840 | tf_op jit(solution)/shard_map/all_gather | solution.py:370
  83.1 0.0 all-to-all-done.1
  83.1 0.0 copy-done
  83.1 3.7 %lag_transform.1 = f32[2,16,64,256]{3,2,1,0:T(8,128)} custom-call(s32[3]{0:T(128)S(1)} %pad_add_fusion.info_ref, bf16[400,512]{1,0:T(8,128)(2,1)S(1)} %copy-done, bf16[6144,128]{1,0:T(8,128)(2,1)S(1)} %bitcast.11, bf16[4,4,32,128]{3,2,1,0:T(8,128)(2,1)S(1)} %bitcast.12, bf16[4,4,32,128]{3,2,1,0:T(8,128)(2,1)S(1)} %bitcast.13), custom_call_target="tpu_custom_call" | custom-call | flops 838860800 | bytes 4194304 | tf_op jit(solution)/shard_map/lag_transform/pallas_call | solution.py:336
Async XLA Ops:
  43.7 3.6 %collective-permute-start = (bf16[256,1024]{1,0:T(8,128)(2,1)S(1)}, bf16[256,1024]{1,0:T(8,128)(2,1)S(1)}, u32[]{:S(2)}, u32[]{:S(2)}) collective-permute-start(bf16[256,1024]{1,0:T(8,128)(2,1)S(1)} %get-tuple-element.15.own_ref), channel_id=1, source_target_pairs={{0,1},{1,0},{2,3},{3,2},{4,5},{5,4},{6,7},{7,6},{8,9},{9,8},{10,11... | collective-permute-start | bytes 1572872 | tf_op jit(solution)/shard_map/ppermute | solution.py:366
  49.9 33.3 %copy-start = (bf16[400,512]{1,0:T(8,128)(2,1)S(1)}, bf16[400,512]{1,0:T(8,128)(2,1)}, u32[]{:S(2)}) copy-start(bf16[400,512]{1,0:T(8,128)(2,1)} %constant.28.clone.table_ref) | copy-start | bytes 1228804
  49.9 33.3 %all-to-all-start.1 = ((bf16[128,48,128]{2,1,0:T(8,128)(2,1)}), bf16[128,48,128]{2,1,0:T(8,128)(2,1)S(1)}, u32[]{:S(2)}, u32[]{:S(2)}) async-start(bf16[128,48,128]{2,1,0:T(8,128)(2,1)} %stack_shared.1), calls=%async_computation.1 | async-start | bytes 3145728 | tf_op jit(solution)/shard_map/all_to_all | solution.py:359
  57.6 20.1 %collective-permute-start.1 = (bf16[4,32,128]{2,1,0:T(8,128)(2,1)S(1)}, bf16[4,32,128]{2,1,0:T(8,128)(2,1)S(1)}, u32[]{:S(2)}, u32[]{:S(2)}) collective-permute-start(bf16[4,32,128]{2,1,0:T(8,128)(2,1)S(1)} %get-tuple-element.20), channel_id=1, source_target_pairs={{0,4},{4,0},{8,12},{12,8},{16,20},{20,16},{24,28},{28,24},{32,36},... | collective-permute-start | bytes 98312 | tf_op jit(solution)/shard_map/ppermute | solution.py:368

commit v5 on v4

--- a/solution.py
+++ b/solution.py
@@ -18,6 +18,7 @@
 WINDOWS = 256
 GROUP = 8
 REACH = 384
+LANES = 896
 
 
 def cos_sin(freqs, times):
@@ -82,9 +83,8 @@
     place = lax.broadcasted_iota(jnp.int32, (BINS, 1), 0)
     count = jnp.minimum(place + 4, BINS - 1) - jnp.maximum(place - 4, 0) + 1
     weight = 1.0 / count.astype(jnp.float32)
-    for part in range(2):
-        for half in range(2):
-            rows_ref[4 * half + 3, pl.ds(6 + part, devices, stride=8), :] = jnp.zeros((devices, 128), jnp.float32)
+    for r in (6, 7):
+        rows_ref[6, pl.ds(r, devices, stride=8), :] = jnp.zeros((devices, 128), jnp.float32)
     dft_ref[...] = dft_rows()
     for w in range(windows):
         copies[w].wait()
@@ -101,17 +101,17 @@
         for part, values in enumerate((real_part * scale, imag_part * scale)):
             for n in range(channels // 128):
                 piece = values[:, n * 128 : (n + 1) * 128]
-                rows_ref[n, pl.ds(part * 2 + w, devices, stride=8), :] = piece[:devices]
-                rows_ref[n, pl.ds(w * 8 + 4 + part, devices // 2, stride=16), :] = piece[devices : BINS - GROUP]
+                place = pl.ds(n // 4 * 4 + part * 2 + w, devices, stride=8)
+                rows_ref[n % 4, place, :] = piece[:devices]
+                place = pl.ds(w * 8 + n // 2 * 2 + part, devices // 2, stride=16)
+                rows_ref[4 + n % 2, place, :] = piece[devices : BINS - GROUP]
             last = values[BINS - GROUP :]
-            last = jnp.concatenate([last, jnp.zeros((GROUP, REACH), jnp.float32)], axis=1)
-            for g in range(devices // GROUP):
-                begin = g * (channels * GROUP // devices)
-                reach = last[:, begin : begin + REACH]
+            last = jnp.concatenate([last, jnp.zeros((GROUP, REACH - 128), jnp.float32)], axis=1)
+            for g in range(devices // (2 * GROUP)):
                 for n in range(REACH // 128):
-                    where = pl.ds(g * GROUP * 8 + 6 + part, GROUP, stride=8)
-                    rows_ref[4 * w + n, where, :] = reach[:, n * 128 : (n + 1) * 128]
-    for n in range(channels // 128):
+                    place = pl.ds(g * 16 * GROUP + w * 8 + n * 2 + part, GROUP, stride=16)
+                    rows_ref[6, place, :] = last[:, (g + n) * 128 : (g + n + 1) * 128]
+    for n in range(rows_ref.shape[0]):
         out_ref[:, n * 128 : (n + 1) * 128] = rows_ref[n].astype(jnp.bfloat16)
 
 
@@ -122,11 +122,11 @@
         functools.partial(whiten_kernel, devices),
         in_specs=[pl.BlockSpec(memory_space=pltpu.HBM)],
         out_specs=pl.BlockSpec(memory_space=pltpu.VMEM),
-        out_shape=jax.ShapeDtypeStruct((rows, channels), jnp.bfloat16),
+        out_shape=jax.ShapeDtypeStruct((rows, LANES), jnp.bfloat16),
         scratch_shapes=[
             pltpu.VMEM(records.shape, jnp.bfloat16),
             pltpu.VMEM((2 * BINS, samples), jnp.bfloat16),
-            pltpu.VMEM((channels // 128, rows, 128), jnp.float32),
+            pltpu.VMEM((LANES // 128, rows, 128), jnp.float32),
             pltpu.SemaphoreType.DMA((windows,)),
         ],
         compiler_params=params(50),
@@ -139,39 +139,6 @@
     row = lax.broadcasted_iota(jnp.int32, (1, 8, even.shape[2]), 1)
     first = row // gap % 2 == 0
     return jnp.where(first, even, pltpu.roll(odd, gap, 1)), jnp.where(first, pltpu.roll(even, 8 - gap, 1), odd)
-
-
-def compact_kernel(rows_ref, own_ref, shared_ref, last_ref):
-    row_count, channels = rows_ref.shape
-    block = 256
-
-    def halves(value):
-        value = value.reshape(value.shape[0] // 2, 2, 8, block)
-        return value[:, 0], value[:, 1]
-
-    for begin in range(0, channels, block):
-        now = slice(begin, begin + block)
-        wide = rows_ref[:, now].astype(jnp.float32).reshape(row_count // 8, 8, block)
-        own, rest = split_rows(*halves(wide), 4)
-        shared, last = split_rows(*halves(rest), 2)
-        for ref, value, gap in ((own_ref, own, 2), (shared_ref, shared, 1), (last_ref, last, 1)):
-            for part, piece in enumerate(split_rows(*halves(value), gap)):
-                count = ref.shape[0] // 2
-                ref[part * count : (part + 1) * count, now] = piece.reshape(count, block).astype(jnp.bfloat16)
-
-
-def compact(rows):
-    row_count, channels = rows.shape
-    shapes = [row_count // 2, row_count // 4, row_count // 4]
-    return pl.pallas_call(
-        compact_kernel,
-        out_shape=[jax.ShapeDtypeStruct((n, channels), jnp.bfloat16) for n in shapes],
-        in_specs=[pl.BlockSpec(memory_space=pltpu.VMEM)],
-        out_specs=[pl.BlockSpec(memory_space=pltpu.VMEM)] * 3,
-        compiler_params=params(16),
-        cost_estimate=cost(0, 4 * 1024 * 1024),
-        name="compact",
-    )(rows)
 
 
 def flip_matrix(count, width):
@@ -208,57 +175,86 @@
         skew_store(part, 257 + 32 * (i % 4), lane, store)
 
 
-def band_products(left, right_ref, begin, width):
-    extent = min(width, right_ref.shape[1] - begin)
+def band_products(left, right_ref, begin, width, channels):
+    extent = min(width, channels - begin)
     products = dot(left, right_ref[:, begin : begin + extent], 1, 0)
     if extent < width:
         products = jnp.concatenate([products, jnp.zeros((left.shape[0], width - extent), jnp.float32)], axis=1)
     return products
 
 
-def stack_kernel(info_ref, own_ref, last_ref, out_ref, mine_ref, pair_ref, rest_ref):
+def compact_kernel(rows_ref, own_ref, shared_ref):
+    row_count = rows_ref.shape[0]
+    channels = own_ref.shape[1]
+
+    def halves(value):
+        value = value.reshape(value.shape[0] // 2, 2, 8, value.shape[2])
+        return value[:, 0], value[:, 1]
+
+    def load(begin, width):
+        return rows_ref[:, begin : begin + width].astype(jnp.float32).reshape(row_count // 8, 8, width)
+
+    def store(ref, value, gap, begin):
+        count, width = ref.shape[0] // 2, value.shape[2]
+        for part, piece in enumerate(split_rows(*halves(value), gap)):
+            where = slice(part * count, (part + 1) * count)
+            ref[where, begin : begin + width] = piece.reshape(count, width).astype(jnp.bfloat16)
+
+    for begin, width, target in ((512, 256, 0), (768, 128, channels)):
+        quarter = 0
+        for value in split_rows(*halves(load(begin, width)), 4):
+            for piece in split_rows(*halves(value), 2):
+                if target + quarter * width < shared_ref.shape[1]:
+                    store(shared_ref, piece, 1, target + quarter * width)
+                quarter += 1
+    for begin in (0, 256):
+        for h, value in enumerate(split_rows(*halves(load(begin, 256)), 4)):
+            store(own_ref, value, 2, h * 512 + begin)
+
+
+def compact(rows, channels):
+    row_count = rows.shape[0]
+    shapes = [(row_count // 2, channels), (row_count // 4, channels + REACH)]
+    return pl.pallas_call(
+        compact_kernel,
+        out_shape=[jax.ShapeDtypeStruct(shape, jnp.bfloat16) for shape in shapes],
+        in_specs=[pl.BlockSpec(memory_space=pltpu.VMEM)],
+        out_specs=[pl.BlockSpec(memory_space=pltpu.VMEM)] * 2,
+        compiler_params=params(16),
+        cost_estimate=cost(0, 4 * 1024 * 1024),
+        name="compact",
+    )(rows)
+
+
+def stack_kernel(own_ref, out_ref):
     row_count, channels = own_ref.shape
     block = 256
     lane = lax.broadcasted_iota(jnp.int32, (16, 128), 1)
-    wide = jnp.concatenate([last_ref[:, :REACH], last_ref[:, 512 : 512 + REACH]], axis=0)
-    left = dot(flip_matrix(64, 128), wide[:, :128], 1, 1).astype(jnp.bfloat16)
-    left = jnp.concatenate([left, turned(left, row_count // 4)], axis=0)
-    products = dot(left, wide, 1, 0)
-    for p in range(2):
-        for i in range(2):
-
-            def store(j, value, p=p, i=i):
-                rest_ref[jnp.where(info_ref[1] == 1 - i, 0, 1), j, p * 16 : (p + 1) * 16, :] = value
-
-            r = p * 64 + i * 32
-            skew_store(products[r : r + 32], REACH - 63 + 32 * i, lane, store)
-    mine_ref[...] = rest_ref[0]
-    pair_ref[...] = rest_ref[1]
     flip = flip_matrix(block, block)
     for c in range(channels // block):
         left = dot(flip, own_ref[:, c * block : (c + 1) * block], 1, 1).astype(jnp.bfloat16)
         left = jnp.concatenate([left, turned(left, row_count // 2)], axis=0)
-        products = band_products(left, own_ref, c * block, 2 * block)
+        products = band_products(left, own_ref, c * block, 2 * block, channels)
         for p in range(2):
             store_items(products[p * block : (p + 1) * block], c, p, out_ref, lane)
 
 
-def stack(info, own, last, devices):
-    shapes = [(devices, 32, 128), (4, 32, 128), (4, 32, 128)]
+def stack(own, devices):
     return pl.pallas_call(
         stack_kernel,
-        out_shape=[jax.ShapeDtypeStruct(shape, jnp.bfloat16) for shape in shapes],
-        in_specs=[pl.BlockSpec(memory_space=pltpu.SMEM)] + [pl.BlockSpec(memory_space=pltpu.VMEM)] * 2,
-        out_specs=[pl.BlockSpec(memory_space=pltpu.VMEM)] * 3,
-        scratch_shapes=[pltpu.VMEM((2, 4, 32, 128), jnp.bfloat16)],
+        out_shape=jax.ShapeDtypeStruct((devices, 32, 128), jnp.bfloat16),
+        in_specs=[pl.BlockSpec(memory_space=pltpu.VMEM)],
+        out_specs=pl.BlockSpec(memory_space=pltpu.VMEM),
         compiler_params=params(16),
         cost_estimate=cost(4 * 1024 * 512 * 512, 4 * 1024 * 1024),
         name="stack",
-    )(info, own, last)
-
-
-def shared_kernel(info_ref, own_ref, other_ref, items_ref, out_hbm, both_ref, item_ref, sems):
-    row_count, channels = own_ref.shape
+    )(own)
+
+
+def shared_kernel(info_ref, own_ref, other_ref, items_ref, out_hbm, *refs):
+    rest_refs, (both_ref, item_ref, rest_ref, sems) = refs[:4], refs[4:]
+    row_count, width = own_ref.shape
+    channels = width - REACH
     block = 256
     copies = [pltpu.make_async_copy(items_ref, out_hbm.at[:, pl.ds(0, 32)], sems.at[0])]
     copies[0].start()
@@ -266,32 +262,46 @@
     both_ref[:row_count] = own_ref[...]
     both_ref[row_count:] = other_ref[...]
     core = info_ref[0]
+
+    def left_side(flip, begin):
+        left = dot(flip, both_ref[:, begin : begin + flip.shape[0]], 1, 1).astype(jnp.bfloat16)
+        return jnp.where(core == 0, left, turned(left, row_count // 2))
+
     flip = flip_matrix(block, block)
     for c in range(channels // block):
-        left = dot(flip, both_ref[:, c * block : (c + 1) * block], 1, 1).astype(jnp.bfloat16)
-        left = jnp.where(core == 0, left, turned(left, row_count // 2))
-        products = band_products(left, both_ref, c * block, 2 * block)
+        products = band_products(left_side(flip, c * block), both_ref, c * block, 2 * block, channels)
         store_items(products, c, 0, item_ref, lane)
         where = pl.ds(c * 32, 32)
         copies.append(
             pltpu.make_async_copy(item_ref.at[where], out_hbm.at[where, pl.ds(32, 16)], sems.at[c + 1])
         )
         copies[-1].start()
+    products = dot(left_side(flip_matrix(128, 128), channels), both_ref[:, channels:], 1, 0)
+    for i in range(4):
+
+        def store(j, value, i=i):
+            rest_ref[jnp.bitwise_and(7 - i - info_ref[1], 3), j] = value
+
+        skew_store(products[i * 32 : (i + 1) * 32], 257 + 32 * i, lane, store)
+    for n, ref in enumerate(rest_refs):
+        ref[...] = rest_ref[n]
     for copy in copies:
         copy.wait()
 
 
 def stack_shared(info, own, other, items, devices):
-    row_count, channels = own.shape
+    row_count, width = own.shape
+    shapes = [(devices, 48, 128)] + [(4, 16, 128)] * 4
     return pl.pallas_call(
         shared_kernel,
-        out_shape=jax.ShapeDtypeStruct((devices, 48, 128), jnp.bfloat16),
+        out_shape=[jax.ShapeDtypeStruct(shape, jnp.bfloat16) for shape in shapes],
         in_specs=[pl.BlockSpec(memory_space=pltpu.SMEM)] + [pl.BlockSpec(memory_space=pltpu.VMEM)] * 3,
-        out_specs=pl.BlockSpec(memory_space=pltpu.HBM),
+        out_specs=[pl.BlockSpec(memory_space=pltpu.HBM)] + [pl.BlockSpec(memory_space=pltpu.VMEM)] * 4,
         scratch_shapes=[
-            pltpu.VMEM((2 * row_count, channels), jnp.bfloat16),
+            pltpu.VMEM((2 * row_count, width), jnp.bfloat16),
             pltpu.VMEM((devices, 16, 128), jnp.bfloat16),
-            pltpu.SemaphoreType.DMA((1 + channels // 256,)),
+            pltpu.VMEM((4, 4, 16, 128), jnp.bfloat16),
+            pltpu.SemaphoreType.DMA((1 + (width - REACH) // 256,)),
         ],
         compiler_params=params(16),
         cost_estimate=cost(2 * 1024 * 512 * 512, 4 * 1024 * 1024),
@@ -299,16 +309,16 @@
     )(info, own, other, items)
 
 
-def lag_kernel(parts, info_ref, table_ref, stacks_ref, mine_ref, pair_ref, out_hbm, wide_ref, out_ref, sems):
+def lag_kernel(parts, info_ref, table_ref, stacks_ref, rest_ref, out_hbm, wide_ref, out_ref, sems):
     items = table_ref.shape[0]
     each = 16 // parts
     split = stacks_ref.shape[0]
     wide_ref[:split] = stacks_ref[...].astype(jnp.float32)
-    mine, win = info_ref[1], info_ref[2]
-    for half, ref in ((mine, mine_ref), (1 - mine, pair_ref)):
+    for k in range(4):
+        source = jnp.bitwise_and(info_ref[1] + 4 - k, 3)
         for n in range(4):
-            begin = pl.multiple_of(split + (half * 4 + n) * 32, 32)
-            wide_ref[pl.ds(begin, 32), :] = ref[n, win].astype(jnp.float32)
+            begin = pl.multiple_of(split + (source * 4 + n) * 16, 16)
+            wide_ref[pl.ds(begin, 16), :] = rest_ref[n, k * 4 + info_ref[2]].astype(jnp.float32)
     swap = info_ref[0]
     copies = []
     for part in range(parts):
@@ -329,13 +339,13 @@
         copy.wait()
 
 
-def lag_transform(info, stacks, mine, pair, devices):
+def lag_transform(info, stacks, rest, devices):
     parts = 8
     table = jnp.asarray(lag_rows(devices))
     shape = (2, 16, 64, LAGS)
     out = pl.pallas_call(
         functools.partial(lag_kernel, parts),
-        in_specs=[pl.BlockSpec(memory_space=pltpu.SMEM)] + [pl.BlockSpec(memory_space=pltpu.VMEM)] * 4,
+        in_specs=[pl.BlockSpec(memory_space=pltpu.SMEM)] + [pl.BlockSpec(memory_space=pltpu.VMEM)] * 3,
         out_specs=pl.BlockSpec(memory_space=pltpu.HBM),
         out_shape=jax.ShapeDtypeStruct(shape, jnp.float32),
         scratch_shapes=[
@@ -346,7 +356,7 @@
         compiler_params=params(24),
         cost_estimate=cost(4 * 2 * BINS * 2048 * 256, 4 * 1024 * 1024),
         name="lag_transform",
-    )(info, table, stacks, mine, pair)
+    )(info, table, stacks, rest)
     return out.reshape(32, 64, LAGS)
 
 
@@ -358,18 +368,18 @@
     def exchange(array):
         return lax.all_to_all(array, axes, split_axis=0, concat_axis=0, tiled=True)
 
-    win = lax.axis_index("win")
-    info = jnp.stack([win % 2, lax.axis_index("chan") % 2, win]).astype(jnp.int32)
-    rows = whiten(records, devices).reshape(devices, 8, channels)
+    chan, win = lax.axis_index("chan"), lax.axis_index("win")
+    info = jnp.stack([win % 2, chan % 4, win]).astype(jnp.int32)
+    rows = whiten(records, devices).reshape(devices, 8, LANES)
     rows, info = lax.optimization_barrier((rows, info))
-    own, shared, last = compact(exchange(rows).reshape(devices * 8, channels))
+    own, shared = compact(exchange(rows).reshape(devices * 8, LANES), channels)
     other = lax.ppermute(shared, "win", [(w, w ^ 1) for w in range(win_size)])
-    items, mine, pair = stack(info, own, last, devices)
-    pair = lax.ppermute(pair, "chan", [(c, c ^ 1) for c in range(chan_size)])
-    mine = lax.all_gather(mine, "win")
-    pair = lax.all_gather(pair, "win")
-    stacks = exchange(stack_shared(info, shared, other, items, devices))
-    return lag_transform(info, stacks.reshape(devices * 48, 128), mine, pair, devices)
+    items = stack(own, devices)
+    stacks, *rest = stack_shared(info, shared, other, items, devices)
+    for n in range(1, 4):
+        rest[n] = lax.ppermute(rest[n], "chan", [(c, c // 4 * 4 + (c + n) % 4) for c in range(chan_size)])
+    rest = lax.all_gather(jnp.concatenate(rest), "win")
+    return lag_transform(info, exchange(stacks).reshape(devices * 48, 128), rest, devices)
 
 
 def solution(mesh):

time: 87.5 us -> 85.4 us (0.976)
  blocking collectives: 60.9 us -> 40.2 us
  waiting for transfers between devices: 0.01 us -> 15.9 us
  starting transfers between devices: 10.2 us -> 14.3 us
  Pallas kernels: 15.6 us -> 14.6 us
    all_gather x2 -> x1, blocking collectives: 24 us -> 6.27 us  [per_device(): rest = lax.all_gather(jnp.concatenate(rest), 'win')]
    ppermute x1 -> x3, waiting for transfers between devices: 0.01 us -> 15.9 us  [per_device(): lax.ppermute(rest[n], 'chan', [(c, c // 4 * 4 + (c + n) % 4) for c in ran...]
    ppermute x1 -> x3, starting transfers between devices: 1.53 us -> 5.37 us  [per_device(): lax.ppermute(rest[n], 'chan', [(c, c // 4 * 4 + (c + n) % 4) for c in ran...]
    all_to_all x1, blocking collectives: 36.9 us -> 34 us  [exchange(): return lax.all_to_all(array, axes, split_axis=0, concat_axis=0, tiled=True)]
  transfers between devices with their start and end apart: 3 -> 5, of which waited for: 0 -> 1; matrix products, arithmetic and copies ran while one was open for 0% -> 0% of each run, Pallas kernels for 3% -> 2%
where the time goes in v5:
time: 85.4 us; the launch traced here: 85.2 us
  blocking collectives  40.2 us (47%)
  waiting for transfers between devices  15.9 us (19%)
  Pallas kernels  14.6 us (17%)
  starting transfers between devices  14.3 us (17%)
    all_to_all x1, blocking collectives, exchange(): return lax.all_to_all(array, axes, split_axis=0, concat_axis=0, tiled=True)  34 us
    ppermute x3, waiting for transfers between devices, per_device(): lax.ppermute(rest[n], 'chan', [(c, c // 4 * 4 + (c + n) % 4) for c in ran...  15.9 us
    all_to_all x1, starting transfers between devices, exchange(): return lax.all_to_all(array, axes, split_axis=0, concat_axis=0, tiled=True)  7.96 us
    all_gather x1, blocking collectives, per_device(): rest = lax.all_gather(jnp.concatenate(rest), 'win')  6.27 us
    ppermute x3, starting transfers between devices, per_device(): lax.ppermute(rest[n], 'chan', [(c, c // 4 * 4 + (c + n) % 4) for c in ran...  5.37 us
    pallas_call x1, Pallas kernels, whiten(): pl.pallas_call(functools.partial(whiten_kernel, devices), in_specs=[pl.Bl...  5.35 us
    pallas_call x1, Pallas kernels, lag_transform(): pl.pallas_call(functools.partial(lag_kernel, parts), in_specs=[pl.BlockSp...  3.68 us
    pallas_call x1, Pallas kernels, stack_shared(): pl.pallas_call(shared_kernel, out_shape=[jax.ShapeDtypeStruct(shape, jnp....  2.65 us
  transfers between devices with their start and end apart: 5, of which 1 were waited for; matrix products, arithmetic and copies ran while one was open for 0% of the time, Pallas kernels for 2%

profile of v5, /device:TPU:21, one launch (start us, length us, event | category | flops | bytes accessed | tf_op | source)
XLA Modules:
  0.0 85.2 jit_solution(13559697110262193119)
XLA Ops:
  0.0 5.3 %whiten.1 = bf16[1024,896]{1,0:T(8,128)(2,1)S(1)} custom-call(bf16[2,1000,1024]{2,1,0:T(8,128)(2,1)} %records_hbm.1), custom_call_target="tpu_custom_call" | custom-call | flops 1638400000 | bytes 6193152 | tf_op jit(solution)/shard_map/whiten/pallas_call | solution.py:121
  5.4 0.1 pad_add_fusion.info_ref
  5.4 34.0 %all_to_all.10 = bf16[128,8,896]{2,1,0:T(8,128)(2,1)S(1)} all-to-all(bf16[128,8,896]{2,1,0:T(8,128)(2,1)S(1)} %bitcast.10), channel_id=1, replica_groups=mesh['chan'=32,'win'=4] {'chan','win'}, dimensions={0} | all-to-all | bytes 3670016 | tf_op jit(solution)/shard_map/all_to_all | solution.py:369
  39.4 1.0 %compact.1 = (bf16[512,1024]{1,0:T(8,128)(2,1)S(1)}, bf16[256,1408]{1,0:T(8,128)(2,1)S(1)}) custom-call(bf16[1024,896]{1,0:T(8,128)(2,1)S(1)} %bitcast.8), custom_call_target="tpu_custom_call" | custom-call | bytes 4194304 | tf_op jit(solution)/shard_map/compact/pallas_call | solution.py:218
  40.4 1.0 %collective-permute-start = (bf16[256,1408]{1,0:T(8,128)(2,1)S(1)}, bf16[256,1408]{1,0:T(8,128)(2,1)S(1)}, u32[]{:S(2)}, u32[]{:S(2)}) collective-permute-start(bf16[256,1408]{1,0:T(8,128)(2,1)S(1)} %get-tuple-element.16.own_ref), channel_id=1, source_target_pairs={{0,1},{1,0},{2,3},{3,2},{4,5},{5,4},{6,7},{7,6},{8,9},{9,8},{10,11... | collective-permute-start | bytes 2162696 | tf_op jit(solution)/shard_map/ppermute | solution.py:376
  41.4 2.0 %stack.17.items_ref = bf16[128,32,128]{2,1,0:T(8,128)(2,1)S(1)} custom-call(bf16[512,1024]{1,0:T(8,128)(2,1)S(1)} %get-tuple-element.17.own_ref), custom_call_target="tpu_custom_call" | custom-call | flops 1073741824 | bytes 4194304 | tf_op jit(solution)/shard_map/stack/pallas_call | solution.py:243
  43.4 0.0 collective-permute-done.other_ref
  43.4 2.6 %stack_shared.1 = (bf16[128,48,128]{2,1,0:T(8,128)(2,1)}, bf16[4,16,128]{2,1,0:T(8,128)(2,1)S(1)}, bf16[4,16,128]{2,1,0:T(8,128)(2,1)S(1)}, bf16[4,16,128]{2,1,0:T(8,128)(2,1)S(1)}, bf16[4,16,128]{2,1,0:T(8,128)(2,1)S(1)}) custom-call(s32[3]{0:T(128)S(1)} %pad_add_fusion.info_ref, bf16[256,1408]{1,0:T(8,128)(2,1)S(1)} %get-tuple-element.16.own_ref, ...), custom_call_target="tpu_custom_call" | custom-call | flops 536870912 | bytes 4194304 | tf_op jit(solution)/shard_map/stack_shared/pallas_call | solution.py:295
  46.0 0.0 copy-start
  46.0 8.0 %all-to-all-start.1 = ((bf16[128,48,128]{2,1,0:T(8,128)(2,1)}), bf16[128,48,128]{2,1,0:T(8,128)(2,1)S(1)}, u32[]{:S(2)}, u32[]{:S(2)}) async-start(bf16[128,48,128]{2,1,0:T(8,128)(2,1)} %get-tuple-element.18), calls=%async_computation.1 | async-start | bytes 3145728 | tf_op jit(solution)/shard_map/all_to_all | solution.py:369
  54.0 1.5 %collective-permute-start.1 = (bf16[4,16,128]{2,1,0:T(8,128)(2,1)S(1)}, bf16[4,16,128]{2,1,0:T(8,128)(2,1)S(1)}, u32[]{:S(2)}, u32[]{:S(2)}) collective-permute-start(bf16[4,16,128]{2,1,0:T(8,128)(2,1)S(1)} %get-tuple-element.20), channel_id=1, source_target_pairs={{0,4},{4,8},{8,12},{12,0},{16,20},{20,24},{24,28},{28,16},{32,36},... | collective-permute-start | bytes 49160 | tf_op jit(solution)/shard_map/ppermute | solution.py:380
  55.5 2.9 %collective-permute-start.2 = (bf16[4,16,128]{2,1,0:T(8,128)(2,1)S(1)}, bf16[4,16,128]{2,1,0:T(8,128)(2,1)S(1)}, u32[]{:S(2)}, u32[]{:S(2)}) collective-permute-start(bf16[4,16,128]{2,1,0:T(8,128)(2,1)S(1)} %get-tuple-element.21), channel_id=1, source_target_pairs={{0,8},{4,12},{8,0},{12,4},{16,24},{20,28},{24,16},{28,20},{32,40},... | collective-permute-start | bytes 49160 | tf_op jit(solution)/shard_map/ppermute | solution.py:380
  58.5 0.9 %collective-permute-start.3 = (bf16[4,16,128]{2,1,0:T(8,128)(2,1)S(1)}, bf16[4,16,128]{2,1,0:T(8,128)(2,1)S(1)}, u32[]{:S(2)}, u32[]{:S(2)}) collective-permute-start(bf16[4,16,128]{2,1,0:T(8,128)(2,1)S(1)} %get-tuple-element.22), channel_id=1, source_target_pairs={{0,12},{4,0},{8,4},{12,8},{16,28},{20,16},{24,20},{28,24},{32,44},... | collective-permute-start | bytes 49160 | tf_op jit(solution)/shard_map/ppermute | solution.py:380
  59.4 15.8 %collective-permute-done.1 = bf16[4,16,128]{2,1,0:T(8,128)(2,1)S(1)} collective-permute-done((bf16[4,16,128]{2,1,0:T(8,128)(2,1)S(1)}, bf16[4,16,128]{2,1,0:T(8,128)(2,1)S(1)}, u32[]{:S(2)}, u32[]{:S(2)}) %collective-permute-start.1) | collective-permute-done | bytes 16416 | tf_op jit(solution)/shard_map/ppermute | solution.py:380
  75.2 0.0 collective-permute-done.2
  75.2 0.0 collective-permute-done.3
  75.3 6.3 %all-gather = bf16[64,16,128]{2,1,0:T(8,128)(2,1)S(1)} all-gather(bf16[16,16,128]{2,1,0:T(8,128)(2,1)S(1)} %pad_maximum_fusion), channel_id=2, replica_groups=mesh['chan'=32,'win'=4] {'win'}, dimensions={0}, use_global_device_ids=true | all-gather | bytes 327680 | tf_op jit(solution)/shard_map/all_gather | solution.py:381
  81.5 0.0 all-to-all-done.1
  81.5 0.0 copy-done
  81.5 3.7 %lag_transform.1 = f32[2,16,64,256]{3,2,1,0:T(8,128)} custom-call(s32[3]{0:T(128)S(1)} %pad_add_fusion.info_ref, bf16[400,512]{1,0:T(8,128)(2,1)S(1)} %copy-done, bf16[6144,128]{1,0:T(8,128)(2,1)S(1)} %bitcast.9, bf16[4,16,16,128]{3,2,1,0:T(8,128)(2,1)S(1)} %bitcast.11), custom_call_target="tpu_custom_call" | custom-call | flops 838860800 | bytes 4194304 | tf_op jit(solution)/shard_map/lag_transform/pallas_call | solution.py:346
  (1 shorter events, 0.0 us)
Async XLA Ops:
  40.4 3.0 %collective-permute-start = (bf16[256,1408]{1,0:T(8,128)(2,1)S(1)}, bf16[256,1408]{1,0:T(8,128)(2,1)S(1)}, u32[]{:S(2)}, u32[]{:S(2)}) collective-permute-start(bf16[256,1408]{1,0:T(8,128)(2,1)S(1)} %get-tuple-element.16.own_ref), channel_id=1, source_target_pairs={{0,1},{1,0},{2,3},{3,2},{4,5},{5,4},{6,7},{7,6},{8,9},{9,8},{10,11... | collective-permute-start | bytes 2162696 | tf_op jit(solution)/shard_map/ppermute | solution.py:376
  46.0 35.5 %copy-start = (bf16[400,512]{1,0:T(8,128)(2,1)S(1)}, bf16[400,512]{1,0:T(8,128)(2,1)}, u32[]{:S(2)}) copy-start(bf16[400,512]{1,0:T(8,128)(2,1)} %constant.34.clone.table_ref) | copy-start | bytes 1228804
  46.0 35.5 %all-to-all-start.1 = ((bf16[128,48,128]{2,1,0:T(8,128)(2,1)}), bf16[128,48,128]{2,1,0:T(8,128)(2,1)S(1)}, u32[]{:S(2)}, u32[]{:S(2)}) async-start(bf16[128,48,128]{2,1,0:T(8,128)(2,1)} %get-tuple-element.18), calls=%async_computation.1 | async-start | bytes 3145728 | tf_op jit(solution)/shard_map/all_to_all | solution.py:369
  54.0 21.2 %collective-permute-start.1 = (bf16[4,16,128]{2,1,0:T(8,128)(2,1)S(1)}, bf16[4,16,128]{2,1,0:T(8,128)(2,1)S(1)}, u32[]{:S(2)}, u32[]{:S(2)}) collective-permute-start(bf16[4,16,128]{2,1,0:T(8,128)(2,1)S(1)} %get-tuple-element.20), channel_id=1, source_target_pairs={{0,4},{4,8},{8,12},{12,0},{16,20},{20,24},{24,28},{28,16},{32,36},... | collective-permute-start | bytes 49160 | tf_op jit(solution)/shard_map/ppermute | solution.py:380
  55.5 19.7 %collective-permute-start.2 = (bf16[4,16,128]{2,1,0:T(8,128)(2,1)S(1)}, bf16[4,16,128]{2,1,0:T(8,128)(2,1)S(1)}, u32[]{:S(2)}, u32[]{:S(2)}) collective-permute-start(bf16[4,16,128]{2,1,0:T(8,128)(2,1)S(1)} %get-tuple-element.21), channel_id=1, source_target_pairs={{0,8},{4,12},{8,0},{12,4},{16,24},{20,28},{24,16},{28,20},{32,40},... | collective-permute-start | bytes 49160 | tf_op jit(solution)/shard_map/ppermute | solution.py:380
  58.5 16.8 %collective-permute-start.3 = (bf16[4,16,128]{2,1,0:T(8,128)(2,1)S(1)}, bf16[4,16,128]{2,1,0:T(8,128)(2,1)S(1)}, u32[]{:S(2)}, u32[]{:S(2)}) collective-permute-start(bf16[4,16,128]{2,1,0:T(8,128)(2,1)S(1)} %get-tuple-element.22), channel_id=1, source_target_pairs={{0,12},{4,0},{8,4},{12,8},{16,28},{20,16},{24,20},{28,24},{32,44},... | collective-permute-start | bytes 49160 | tf_op jit(solution)/shard_map/ppermute | solution.py:380

commit v6 on v5

--- a/solution.py
+++ b/solution.py
@@ -77,8 +77,9 @@
     for w in range(windows):
         copies.append(pltpu.make_async_copy(records_hbm.at[w], records_ref.at[w], sems.at[w]))
         copies[-1].start()
-    row = lax.broadcasted_iota(jnp.int32, (BINS, BINS), 0)
-    column = lax.broadcasted_iota(jnp.int32, (BINS, BINS), 1)
+    row = lax.broadcasted_iota(jnp.int32, (BINS, 2 * BINS), 0)
+    column = lax.broadcasted_iota(jnp.int32, (BINS, 2 * BINS), 1)
+    column = jnp.where(column < BINS, column, column - BINS)
     near = jnp.where(jnp.abs(row - column) <= 4, 1.0, 0.0).astype(jnp.bfloat16)
     place = lax.broadcasted_iota(jnp.int32, (BINS, 1), 0)
     count = jnp.minimum(place + 4, BINS - 1) - jnp.maximum(place - 4, 0) + 1
@@ -93,9 +94,9 @@
         imag_part = spectra[BINS:]
         power = real_part * real_part + imag_part * imag_part
         size = jnp.sqrt(power)
-        high = size.astype(jnp.bfloat16)
-        low = (size - high.astype(jnp.float32)).astype(jnp.bfloat16)
-        smooth = (dot(near, high, 1, 0) + dot(near, low, 1, 0)) * weight
+        high = size.astype(jnp.bfloat16).astype(jnp.float32)
+        both = jnp.concatenate([high, size - high], axis=0).astype(jnp.bfloat16)
+        smooth = dot(near, both, 1, 0) * weight
         level = jnp.sqrt(jnp.sum(power, axis=0, keepdims=True) * (1.0 / BINS) + 1e-06)
         scale = 1.0 / (smooth + 0.25 * level)
         for part, values in enumerate((real_part * scale, imag_part * scale)):
@@ -309,23 +310,23 @@
     )(info, own, other, items)
 
 
-def lag_kernel(parts, info_ref, table_ref, stacks_ref, rest_ref, out_hbm, wide_ref, out_ref, sems):
-    items = table_ref.shape[0]
+def lag_kernel(parts, info_ref, table_ref, stacks_ref, rest_ref, out_hbm, wide_ref, last_ref, out_ref, sems):
     each = 16 // parts
     split = stacks_ref.shape[0]
-    wide_ref[:split] = stacks_ref[...].astype(jnp.float32)
+    wide_ref[...] = stacks_ref[...].astype(jnp.float32)
     for k in range(4):
         source = jnp.bitwise_and(info_ref[1] + 4 - k, 3)
         for n in range(4):
-            begin = pl.multiple_of(split + (source * 4 + n) * 16, 16)
-            wide_ref[pl.ds(begin, 16), :] = rest_ref[n, k * 4 + info_ref[2]].astype(jnp.float32)
+            begin = pl.multiple_of((source * 4 + n) * 16, 16)
+            last_ref[pl.ds(begin, 16), :] = rest_ref[n, k * 4 + info_ref[2]].astype(jnp.float32)
     swap = info_ref[0]
     copies = []
     for part in range(parts):
         sides = []
         for n in range(each):
             place = 15 - (part * each + n)
-            sides.append(wide_ref[pl.ds(place, items, stride=16), :].astype(jnp.bfloat16))
+            side = [wide_ref[pl.ds(place, split // 16, stride=16), :], last_ref[pl.ds(place, 16, stride=16), :]]
+            sides.append(jnp.concatenate(side, axis=0).astype(jnp.bfloat16))
         both = dot(jnp.concatenate(sides, axis=1), table_ref[...], 0, 0)
         lags = both[:, :LAGS] + both[:, LAGS:]
         for n in range(each):
@@ -349,7 +350,8 @@
         out_specs=pl.BlockSpec(memory_space=pltpu.HBM),
         out_shape=jax.ShapeDtypeStruct(shape, jnp.float32),
         scratch_shapes=[
-            pltpu.VMEM((2 * BINS * 16, 128), jnp.float32),
+            pltpu.VMEM(stacks.shape, jnp.float32),
+            pltpu.VMEM((2 * GROUP * 16, 128), jnp.float32),
             pltpu.VMEM(shape, jnp.float32),
             pltpu.SemaphoreType.DMA((parts,)),
         ],

time: 85.4 us -> 85.2 us (level)
  no operation moved by 1% of the time
where the time goes in v6:
time: 85.2 us; the launch traced here: 85 us
  blocking collectives  40.2 us (47%)
  waiting for transfers between devices  15.9 us (19%)
  Pallas kernels  14.4 us (17%)
  starting transfers between devices  14.3 us (17%)
    all_to_all x1, blocking collectives, exchange(): return lax.all_to_all(array, axes, split_axis=0, concat_axis=0, tiled=True)  34 us
    ppermute x3, waiting for transfers between devices, per_device(): lax.ppermute(rest[n], 'chan', [(c, c // 4 * 4 + (c + n) % 4) for c in ran...  15.9 us
    all_to_all x1, starting transfers between devices, exchange(): return lax.all_to_all(array, axes, split_axis=0, concat_axis=0, tiled=True)  7.96 us
    all_gather x1, blocking collectives, per_device(): rest = lax.all_gather(jnp.concatenate(rest), 'win')  6.27 us
    ppermute x3, starting transfers between devices, per_device(): lax.ppermute(rest[n], 'chan', [(c, c // 4 * 4 + (c + n) % 4) for c in ran...  5.37 us
    pallas_call x1, Pallas kernels, whiten(): pl.pallas_call(functools.partial(whiten_kernel, devices), in_specs=[pl.Bl...  5.13 us
    pallas_call x1, Pallas kernels, lag_transform(): pl.pallas_call(functools.partial(lag_kernel, parts), in_specs=[pl.BlockSp...  3.66 us
    pallas_call x1, Pallas kernels, stack_shared(): pl.pallas_call(shared_kernel, out_shape=[jax.ShapeDtypeStruct(shape, jnp....  2.65 us
  transfers between devices with their start and end apart: 5, of which 1 were waited for; matrix products, arithmetic and copies ran while one was open for 0% of the time, Pallas kernels for 2%

profile of v6, /device:TPU:21, one launch (start us, length us, event | category | flops | bytes accessed | tf_op | source)
XLA Modules:
  0.0 85.0 jit_solution(3108281623780443161)
XLA Ops:
  0.0 5.1 %whiten.1 = bf16[1024,896]{1,0:T(8,128)(2,1)S(1)} custom-call(bf16[2,1000,1024]{2,1,0:T(8,128)(2,1)} %records_hbm.1), custom_call_target="tpu_custom_call" | custom-call | flops 1638400000 | bytes 6193152 | tf_op jit(solution)/shard_map/whiten/pallas_call | solution.py:122
  5.2 0.1 pad_add_fusion.info_ref
  5.2 34.0 %all_to_all.10 = bf16[128,8,896]{2,1,0:T(8,128)(2,1)S(1)} all-to-all(bf16[128,8,896]{2,1,0:T(8,128)(2,1)S(1)} %bitcast.10), channel_id=1, replica_groups=mesh['chan'=32,'win'=4] {'chan','win'}, dimensions={0} | all-to-all | bytes 3670016 | tf_op jit(solution)/shard_map/all_to_all | solution.py:371
  39.2 1.0 %compact.1 = (bf16[512,1024]{1,0:T(8,128)(2,1)S(1)}, bf16[256,1408]{1,0:T(8,128)(2,1)S(1)}) custom-call(bf16[1024,896]{1,0:T(8,128)(2,1)S(1)} %bitcast.8), custom_call_target="tpu_custom_call" | custom-call | bytes 4194304 | tf_op jit(solution)/shard_map/compact/pallas_call | solution.py:219
  40.2 1.0 %collective-permute-start = (bf16[256,1408]{1,0:T(8,128)(2,1)S(1)}, bf16[256,1408]{1,0:T(8,128)(2,1)S(1)}, u32[]{:S(2)}, u32[]{:S(2)}) collective-permute-start(bf16[256,1408]{1,0:T(8,128)(2,1)S(1)} %get-tuple-element.16.own_ref), channel_id=1, source_target_pairs={{0,1},{1,0},{2,3},{3,2},{4,5},{5,4},{6,7},{7,6},{8,9},{9,8},{10,11... | collective-permute-start | bytes 2162696 | tf_op jit(solution)/shard_map/ppermute | solution.py:378
  41.2 2.0 %stack.17.items_ref = bf16[128,32,128]{2,1,0:T(8,128)(2,1)S(1)} custom-call(bf16[512,1024]{1,0:T(8,128)(2,1)S(1)} %get-tuple-element.17.own_ref), custom_call_target="tpu_custom_call" | custom-call | flops 1073741824 | bytes 4194304 | tf_op jit(solution)/shard_map/stack/pallas_call | solution.py:244
  43.1 0.0 collective-permute-done.other_ref
  43.2 2.6 %stack_shared.1 = (bf16[128,48,128]{2,1,0:T(8,128)(2,1)}, bf16[4,16,128]{2,1,0:T(8,128)(2,1)S(1)}, bf16[4,16,128]{2,1,0:T(8,128)(2,1)S(1)}, bf16[4,16,128]{2,1,0:T(8,128)(2,1)S(1)}, bf16[4,16,128]{2,1,0:T(8,128)(2,1)S(1)}) custom-call(s32[3]{0:T(128)S(1)} %pad_add_fusion.info_ref, bf16[256,1408]{1,0:T(8,128)(2,1)S(1)} %get-tuple-element.16.own_ref, ...), custom_call_target="tpu_custom_call" | custom-call | flops 536870912 | bytes 4194304 | tf_op jit(solution)/shard_map/stack_shared/pallas_call | solution.py:296
  45.8 0.0 copy-start
  45.8 8.0 %all-to-all-start.1 = ((bf16[128,48,128]{2,1,0:T(8,128)(2,1)}), bf16[128,48,128]{2,1,0:T(8,128)(2,1)S(1)}, u32[]{:S(2)}, u32[]{:S(2)}) async-start(bf16[128,48,128]{2,1,0:T(8,128)(2,1)} %get-tuple-element.18), calls=%async_computation.1 | async-start | bytes 3145728 | tf_op jit(solution)/shard_map/all_to_all | solution.py:371
  53.8 1.5 %collective-permute-start.1 = (bf16[4,16,128]{2,1,0:T(8,128)(2,1)S(1)}, bf16[4,16,128]{2,1,0:T(8,128)(2,1)S(1)}, u32[]{:S(2)}, u32[]{:S(2)}) collective-permute-start(bf16[4,16,128]{2,1,0:T(8,128)(2,1)S(1)} %get-tuple-element.20), channel_id=1, source_target_pairs={{0,4},{4,8},{8,12},{12,0},{16,20},{20,24},{24,28},{28,16},{32,36},... | collective-permute-start | bytes 49160 | tf_op jit(solution)/shard_map/ppermute | solution.py:382
  55.3 2.9 %collective-permute-start.2 = (bf16[4,16,128]{2,1,0:T(8,128)(2,1)S(1)}, bf16[4,16,128]{2,1,0:T(8,128)(2,1)S(1)}, u32[]{:S(2)}, u32[]{:S(2)}) collective-permute-start(bf16[4,16,128]{2,1,0:T(8,128)(2,1)S(1)} %get-tuple-element.21), channel_id=1, source_target_pairs={{0,8},{4,12},{8,0},{12,4},{16,24},{20,28},{24,16},{28,20},{32,40},... | collective-permute-start | bytes 49160 | tf_op jit(solution)/shard_map/ppermute | solution.py:382
  58.2 0.9 %collective-permute-start.3 = (bf16[4,16,128]{2,1,0:T(8,128)(2,1)S(1)}, bf16[4,16,128]{2,1,0:T(8,128)(2,1)S(1)}, u32[]{:S(2)}, u32[]{:S(2)}) collective-permute-start(bf16[4,16,128]{2,1,0:T(8,128)(2,1)S(1)} %get-tuple-element.22), channel_id=1, source_target_pairs={{0,12},{4,0},{8,4},{12,8},{16,28},{20,16},{24,20},{28,24},{32,44},... | collective-permute-start | bytes 49160 | tf_op jit(solution)/shard_map/ppermute | solution.py:382
  59.2 15.8 %collective-permute-done.1 = bf16[4,16,128]{2,1,0:T(8,128)(2,1)S(1)} collective-permute-done((bf16[4,16,128]{2,1,0:T(8,128)(2,1)S(1)}, bf16[4,16,128]{2,1,0:T(8,128)(2,1)S(1)}, u32[]{:S(2)}, u32[]{:S(2)}) %collective-permute-start.1) | collective-permute-done | bytes 16416 | tf_op jit(solution)/shard_map/ppermute | solution.py:382
  75.0 0.0 collective-permute-done.2
  75.0 0.0 collective-permute-done.3
  75.1 6.3 %all-gather = bf16[64,16,128]{2,1,0:T(8,128)(2,1)S(1)} all-gather(bf16[16,16,128]{2,1,0:T(8,128)(2,1)S(1)} %pad_maximum_fusion), channel_id=2, replica_groups=mesh['chan'=32,'win'=4] {'win'}, dimensions={0}, use_global_device_ids=true | all-gather | bytes 327680 | tf_op jit(solution)/shard_map/all_gather | solution.py:383
  81.3 0.0 all-to-all-done.1
  81.3 0.0 copy-done
  81.3 3.7 %lag_transform.1 = f32[2,16,64,256]{3,2,1,0:T(8,128)} custom-call(s32[3]{0:T(128)S(1)} %pad_add_fusion.info_ref, bf16[400,512]{1,0:T(8,128)(2,1)S(1)} %copy-done, bf16[6144,128]{1,0:T(8,128)(2,1)S(1)} %bitcast.9, bf16[4,16,16,128]{3,2,1,0:T(8,128)(2,1)S(1)} %bitcast.11), custom_call_target="tpu_custom_call" | custom-call | flops 838860800 | bytes 4194304 | tf_op jit(solution)/shard_map/lag_transform/pallas_call | solution.py:347
  (1 shorter events, 0.0 us)
Async XLA Ops:
  40.2 3.0 %collective-permute-start = (bf16[256,1408]{1,0:T(8,128)(2,1)S(1)}, bf16[256,1408]{1,0:T(8,128)(2,1)S(1)}, u32[]{:S(2)}, u32[]{:S(2)}) collective-permute-start(bf16[256,1408]{1,0:T(8,128)(2,1)S(1)} %get-tuple-element.16.own_ref), channel_id=1, source_target_pairs={{0,1},{1,0},{2,3},{3,2},{4,5},{5,4},{6,7},{7,6},{8,9},{9,8},{10,11... | collective-permute-start | bytes 2162696 | tf_op jit(solution)/shard_map/ppermute | solution.py:378
  45.8 35.5 %copy-start = (bf16[400,512]{1,0:T(8,128)(2,1)S(1)}, bf16[400,512]{1,0:T(8,128)(2,1)}, u32[]{:S(2)}) copy-start(bf16[400,512]{1,0:T(8,128)(2,1)} %constant.34.clone.table_ref) | copy-start | bytes 1228804
  45.8 35.5 %all-to-all-start.1 = ((bf16[128,48,128]{2,1,0:T(8,128)(2,1)}), bf16[128,48,128]{2,1,0:T(8,128)(2,1)S(1)}, u32[]{:S(2)}, u32[]{:S(2)}) async-start(bf16[128,48,128]{2,1,0:T(8,128)(2,1)} %get-tuple-element.18), calls=%async_computation.1 | async-start | bytes 3145728 | tf_op jit(solution)/shard_map/all_to_all | solution.py:371
  53.8 21.2 %collective-permute-start.1 = (bf16[4,16,128]{2,1,0:T(8,128)(2,1)S(1)}, bf16[4,16,128]{2,1,0:T(8,128)(2,1)S(1)}, u32[]{:S(2)}, u32[]{:S(2)}) collective-permute-start(bf16[4,16,128]{2,1,0:T(8,128)(2,1)S(1)} %get-tuple-element.20), channel_id=1, source_target_pairs={{0,4},{4,8},{8,12},{12,0},{16,20},{20,24},{24,28},{28,16},{32,36},... | collective-permute-start | bytes 49160 | tf_op jit(solution)/shard_map/ppermute | solution.py:382
  55.3 19.7 %collective-permute-start.2 = (bf16[4,16,128]{2,1,0:T(8,128)(2,1)S(1)}, bf16[4,16,128]{2,1,0:T(8,128)(2,1)S(1)}, u32[]{:S(2)}, u32[]{:S(2)}) collective-permute-start(bf16[4,16,128]{2,1,0:T(8,128)(2,1)S(1)} %get-tuple-element.21), channel_id=1, source_target_pairs={{0,8},{4,12},{8,0},{12,4},{16,24},{20,28},{24,16},{28,20},{32,40},... | collective-permute-start | bytes 49160 | tf_op jit(solution)/shard_map/ppermute | solution.py:382
  58.2 16.8 %collective-permute-start.3 = (bf16[4,16,128]{2,1,0:T(8,128)(2,1)S(1)}, bf16[4,16,128]{2,1,0:T(8,128)(2,1)S(1)}, u32[]{:S(2)}, u32[]{:S(2)}) collective-permute-start(bf16[4,16,128]{2,1,0:T(8,128)(2,1)S(1)} %get-tuple-element.22), channel_id=1, source_target_pairs={{0,12},{4,0},{8,4},{12,8},{16,28},{20,16},{24,20},{28,24},{32,44},... | collective-permute-start | bytes 49160 | tf_op jit(solution)/shard_map/ppermute | solution.py:382

commit v7 on v6

--- a/solution.py
+++ b/solution.py
@@ -184,52 +184,52 @@
     return products
 
 
-def compact_kernel(rows_ref, own_ref, shared_ref):
+def halves(value):
+    value = value.reshape(value.shape[0] // 2, 2, 8, value.shape[2])
+    return value[:, 0], value[:, 1]
+
+
+def load_rows(rows_ref, begin, width):
     row_count = rows_ref.shape[0]
-    channels = own_ref.shape[1]
-
-    def halves(value):
-        value = value.reshape(value.shape[0] // 2, 2, 8, value.shape[2])
-        return value[:, 0], value[:, 1]
-
-    def load(begin, width):
-        return rows_ref[:, begin : begin + width].astype(jnp.float32).reshape(row_count // 8, 8, width)
-
-    def store(ref, value, gap, begin):
-        count, width = ref.shape[0] // 2, value.shape[2]
-        for part, piece in enumerate(split_rows(*halves(value), gap)):
-            where = slice(part * count, (part + 1) * count)
-            ref[where, begin : begin + width] = piece.reshape(count, width).astype(jnp.bfloat16)
-
+    return rows_ref[:, begin : begin + width].astype(jnp.float32).reshape(row_count // 8, 8, width)
+
+
+def store_parts(ref, value, gap, begin):
+    count, width = ref.shape[0] // 2, value.shape[2]
+    for part, piece in enumerate(split_rows(*halves(value), gap)):
+        where = slice(part * count, (part + 1) * count)
+        ref[where, begin : begin + width] = piece.reshape(count, width).astype(jnp.bfloat16)
+
+
+def compact_kernel(channels, rows_ref, shared_ref):
     for begin, width, target in ((512, 256, 0), (768, 128, channels)):
         quarter = 0
-        for value in split_rows(*halves(load(begin, width)), 4):
+        for value in split_rows(*halves(load_rows(rows_ref, begin, width)), 4):
             for piece in split_rows(*halves(value), 2):
                 if target + quarter * width < shared_ref.shape[1]:
-                    store(shared_ref, piece, 1, target + quarter * width)
+                    store_parts(shared_ref, piece, 1, target + quarter * width)
                 quarter += 1
-    for begin in (0, 256):
-        for h, value in enumerate(split_rows(*halves(load(begin, 256)), 4)):
-            store(own_ref, value, 2, h * 512 + begin)
 
 
 def compact(rows, channels):
     row_count = rows.shape[0]
-    shapes = [(row_count // 2, channels), (row_count // 4, channels + REACH)]
     return pl.pallas_call(
-        compact_kernel,
-        out_shape=[jax.ShapeDtypeStruct(shape, jnp.bfloat16) for shape in shapes],
+        functools.partial(compact_kernel, channels),
+        out_shape=jax.ShapeDtypeStruct((row_count // 4, channels + REACH), jnp.bfloat16),
         in_specs=[pl.BlockSpec(memory_space=pltpu.VMEM)],
-        out_specs=[pl.BlockSpec(memory_space=pltpu.VMEM)] * 2,
+        out_specs=pl.BlockSpec(memory_space=pltpu.VMEM),
         compiler_params=params(16),
-        cost_estimate=cost(0, 4 * 1024 * 1024),
+        cost_estimate=cost(0, 2 * 1024 * 1024),
         name="compact",
     )(rows)
 
 
-def stack_kernel(own_ref, out_ref):
+def stack_kernel(rows_ref, out_ref, own_ref):
     row_count, channels = own_ref.shape
     block = 256
+    for begin in (0, 256):
+        for h, value in enumerate(split_rows(*halves(load_rows(rows_ref, begin, 256)), 4)):
+            store_parts(own_ref, value, 2, h * 512 + begin)
     lane = lax.broadcasted_iota(jnp.int32, (16, 128), 1)
     flip = flip_matrix(block, block)
     for c in range(channels // block):
@@ -240,16 +240,17 @@
             store_items(products[p * block : (p + 1) * block], c, p, out_ref, lane)
 
 
-def stack(own, devices):
+def stack(rows, channels, devices):
     return pl.pallas_call(
         stack_kernel,
         out_shape=jax.ShapeDtypeStruct((devices, 32, 128), jnp.bfloat16),
         in_specs=[pl.BlockSpec(memory_space=pltpu.VMEM)],
         out_specs=pl.BlockSpec(memory_space=pltpu.VMEM),
+        scratch_shapes=[pltpu.VMEM((rows.shape[0] // 2, channels), jnp.bfloat16)],
         compiler_params=params(16),
         cost_estimate=cost(4 * 1024 * 512 * 512, 4 * 1024 * 1024),
         name="stack",
-    )(own)
+    )(rows)
 
 
 def shared_kernel(info_ref, own_ref, other_ref, items_ref, out_hbm, *refs):
@@ -346,7 +347,13 @@
     shape = (2, 16, 64, LAGS)
     out = pl.pallas_call(
         functools.partial(lag_kernel, parts),
-        in_specs=[pl.BlockSpec(memory_space=pltpu.SMEM)] + [pl.BlockSpec(memory_space=pltpu.VMEM)] * 3,
+        grid=(1,),
+        in_specs=[
+            pl.BlockSpec(memory_space=pltpu.SMEM),
+            pl.BlockSpec(table.shape, lambda i: (0, 0)),
+            pl.BlockSpec(stacks.shape, lambda i: (0, 0)),
+            pl.BlockSpec(rest.shape, lambda i: (0, 0, 0, 0)),
+        ],
         out_specs=pl.BlockSpec(memory_space=pltpu.HBM),
         out_shape=jax.ShapeDtypeStruct(shape, jnp.float32),
         scratch_shapes=[
@@ -374,9 +381,10 @@
     info = jnp.stack([win % 2, chan % 4, win]).astype(jnp.int32)
     rows = whiten(records, devices).reshape(devices, 8, LANES)
     rows, info = lax.optimization_barrier((rows, info))
-    own, shared = compact(exchange(rows).reshape(devices * 8, LANES), channels)
+    rows = exchange(rows).reshape(devices * 8, LANES)
+    shared = compact(rows, channels)
     other = lax.ppermute(shared, "win", [(w, w ^ 1) for w in range(win_size)])
-    items = stack(own, devices)
+    items = stack(rows, channels, devices)
     stacks, *rest = stack_shared(info, shared, other, items, devices)
     for n in range(1, 4):
         rest[n] = lax.ppermute(rest[n], "chan", [(c, c // 4 * 4 + (c + n) % 4) for c in range(chan_size)])

time: 85.2 us -> 84.7 us (level)
  transfers between devices with their start and end apart: 5 -> 5, of which waited for: 1 -> 1; matrix products, arithmetic and copies ran while one was open for 0% -> 0% of each run, Pallas kernels for 2% -> 3%
where the time goes in v7:
time: 84.7 us; the launch traced here: 84.5 us
  blocking collectives  40.2 us (47%)
  waiting for transfers between devices  15.9 us (19%)
  Pallas kernels  14.1 us (17%)
  starting transfers between devices  14.1 us (17%)
    all_to_all x1, blocking collectives, exchange(): return lax.all_to_all(array, axes, split_axis=0, concat_axis=0, tiled=True)  34 us
    ppermute x3, waiting for transfers between devices, per_device(): lax.ppermute(rest[n], 'chan', [(c, c // 4 * 4 + (c + n) % 4) for c in ran...  15.9 us
    all_to_all x1, starting transfers between devices, exchange(): return lax.all_to_all(array, axes, split_axis=0, concat_axis=0, tiled=True)  7.77 us
    all_gather x1, blocking collectives, per_device(): rest = lax.all_gather(jnp.concatenate(rest), 'win')  6.27 us
    ppermute x3, starting transfers between devices, per_device(): lax.ppermute(rest[n], 'chan', [(c, c // 4 * 4 + (c + n) % 4) for c in ran...  5.37 us
    pallas_call x1, Pallas kernels, whiten(): pl.pallas_call(functools.partial(whiten_kernel, devices), in_specs=[pl.Bl...  5.13 us
    pallas_call x1, Pallas kernels, lag_transform(): pl.pallas_call(functools.partial(lag_kernel, parts), grid=(1,), in_specs=...  3.66 us
    pallas_call x1, Pallas kernels, stack_shared(): pl.pallas_call(shared_kernel, out_shape=[jax.ShapeDtypeStruct(shape, jnp....  2.64 us
  transfers between devices with their start and end apart: 5, of which 1 were waited for; matrix products, arithmetic and copies ran while one was open for 0% of the time, Pallas kernels for 3%

profile of v7, /device:TPU:21, one launch (start us, length us, event | category | flops | bytes accessed | tf_op | source)
XLA Modules:
  0.0 84.5 jit_solution(13854586607444536645)
XLA Ops:
  0.0 5.1 %whiten.1 = bf16[1024,896]{1,0:T(8,128)(2,1)S(1)} custom-call(bf16[2,1000,1024]{2,1,0:T(8,128)(2,1)} %records_hbm.1), custom_call_target="tpu_custom_call" | custom-call | flops 1638400000 | bytes 6193152 | tf_op jit(solution)/shard_map/whiten/pallas_call | solution.py:122
  5.2 0.1 pad_add_fusion.info_ref
  5.2 34.0 %all_to_all.10 = bf16[128,8,896]{2,1,0:T(8,128)(2,1)S(1)} all-to-all(bf16[128,8,896]{2,1,0:T(8,128)(2,1)S(1)} %bitcast.11), channel_id=1, replica_groups=mesh['chan'=32,'win'=4] {'chan','win'}, dimensions={0} | all-to-all | bytes 3670016 | tf_op jit(solution)/shard_map/all_to_all | solution.py:378
  39.2 0.5 compact.1.own_ref
  39.7 1.0 %collective-permute-start = (bf16[256,1408]{1,0:T(8,128)(2,1)S(1)}, bf16[256,1408]{1,0:T(8,128)(2,1)S(1)}, u32[]{:S(2)}, u32[]{:S(2)}) collective-permute-start(bf16[256,1408]{1,0:T(8,128)(2,1)S(1)} %compact.1.own_ref), channel_id=1, source_target_pairs={{0,1},{1,0},{2,3},{3,2},{4,5},{5,4},{6,7},{7,6},{8,9},{9,8},{10,11... | collective-permute-start | bytes 2162696 | tf_op jit(solution)/shard_map/ppermute | solution.py:386
  40.7 2.1 %stack.17.items_ref = bf16[128,32,128]{2,1,0:T(8,128)(2,1)S(1)} custom-call(bf16[1024,896]{1,0:T(8,128)(2,1)S(1)} %bitcast.9), custom_call_target="tpu_custom_call" | custom-call | flops 1073741824 | bytes 4194304 | tf_op jit(solution)/shard_map/stack/pallas_call | solution.py:244
  42.8 0.0 collective-permute-done.other_ref
  42.8 2.6 %stack_shared.1 = (bf16[128,48,128]{2,1,0:T(8,128)(2,1)}, bf16[4,16,128]{2,1,0:T(8,128)(2,1)S(1)}, bf16[4,16,128]{2,1,0:T(8,128)(2,1)S(1)}, bf16[4,16,128]{2,1,0:T(8,128)(2,1)S(1)}, bf16[4,16,128]{2,1,0:T(8,128)(2,1)S(1)}) custom-call(s32[3]{0:T(128)S(1)} %pad_add_fusion.info_ref, bf16[256,1408]{1,0:T(8,128)(2,1)S(1)} %compact.1.own_ref, ...), custom_call_target="tpu_custom_call" | custom-call | flops 536870912 | bytes 4194304 | tf_op jit(solution)/shard_map/stack_shared/pallas_call | solution.py:297
  45.5 0.0 copy-start
  45.5 7.8 %all-to-all-start.1 = ((bf16[128,48,128]{2,1,0:T(8,128)(2,1)}), bf16[128,48,128]{2,1,0:T(8,128)(2,1)S(1)}, u32[]{:S(2)}, u32[]{:S(2)}) async-start(bf16[128,48,128]{2,1,0:T(8,128)(2,1)} %get-tuple-element.14), calls=%async_computation.1 | async-start | bytes 3145728 | tf_op jit(solution)/shard_map/all_to_all | solution.py:378
  53.3 1.5 %collective-permute-start.1 = (bf16[4,16,128]{2,1,0:T(8,128)(2,1)S(1)}, bf16[4,16,128]{2,1,0:T(8,128)(2,1)S(1)}, u32[]{:S(2)}, u32[]{:S(2)}) collective-permute-start(bf16[4,16,128]{2,1,0:T(8,128)(2,1)S(1)} %get-tuple-element.16), channel_id=1, source_target_pairs={{0,4},{4,8},{8,12},{12,0},{16,20},{20,24},{24,28},{28,16},{32,36},... | collective-permute-start | bytes 49160 | tf_op jit(solution)/shard_map/ppermute | solution.py:390
  54.8 2.9 %collective-permute-start.2 = (bf16[4,16,128]{2,1,0:T(8,128)(2,1)S(1)}, bf16[4,16,128]{2,1,0:T(8,128)(2,1)S(1)}, u32[]{:S(2)}, u32[]{:S(2)}) collective-permute-start(bf16[4,16,128]{2,1,0:T(8,128)(2,1)S(1)} %get-tuple-element.17), channel_id=1, source_target_pairs={{0,8},{4,12},{8,0},{12,4},{16,24},{20,28},{24,16},{28,20},{32,40},... | collective-permute-start | bytes 49160 | tf_op jit(solution)/shard_map/ppermute | solution.py:390
  57.7 0.9 %collective-permute-start.3 = (bf16[4,16,128]{2,1,0:T(8,128)(2,1)S(1)}, bf16[4,16,128]{2,1,0:T(8,128)(2,1)S(1)}, u32[]{:S(2)}, u32[]{:S(2)}) collective-permute-start(bf16[4,16,128]{2,1,0:T(8,128)(2,1)S(1)} %get-tuple-element.18), channel_id=1, source_target_pairs={{0,12},{4,0},{8,4},{12,8},{16,28},{20,16},{24,20},{28,24},{32,44},... | collective-permute-start | bytes 49160 | tf_op jit(solution)/shard_map/ppermute | solution.py:390
  58.6 15.8 %collective-permute-done.1 = bf16[4,16,128]{2,1,0:T(8,128)(2,1)S(1)} collective-permute-done((bf16[4,16,128]{2,1,0:T(8,128)(2,1)S(1)}, bf16[4,16,128]{2,1,0:T(8,128)(2,1)S(1)}, u32[]{:S(2)}, u32[]{:S(2)}) %collective-permute-start.1) | collective-permute-done | bytes 16416 | tf_op jit(solution)/shard_map/ppermute | solution.py:390
  74.5 0.0 collective-permute-done.2
  74.5 0.0 collective-permute-done.3
  74.5 6.3 %all-gather = bf16[64,16,128]{2,1,0:T(8,128)(2,1)S(1)} all-gather(bf16[16,16,128]{2,1,0:T(8,128)(2,1)S(1)} %pad_maximum_fusion), channel_id=2, replica_groups=mesh['chan'=32,'win'=4] {'win'}, dimensions={0}, use_global_device_ids=true | all-gather | bytes 327680 | tf_op jit(solution)/shard_map/all_gather | solution.py:391
  80.8 0.0 all-to-all-done.1
  80.8 0.0 copy-done
  80.8 3.7 %lag_transform.1 = f32[2,16,64,256]{3,2,1,0:T(8,128)} custom-call(s32[3]{0:T(128)S(1)} %pad_add_fusion.info_ref, bf16[400,512]{1,0:T(8,128)(2,1)S(1)} %copy-done, bf16[6144,128]{1,0:T(8,128)(2,1)S(1)} %bitcast.10, bf16[4,16,16,128]{3,2,1,0:T(8,128)(2,1)S(1)} %bitcast.12), custom_call_target="tpu_custom_call" | custom-call | flops 838860800 | bytes 4194304 | tf_op jit(solution)/shard_map/lag_transform/pallas_call | solution.py:348
  (1 shorter events, 0.0 us)
Async XLA Ops:
  39.7 3.1 %collective-permute-start = (bf16[256,1408]{1,0:T(8,128)(2,1)S(1)}, bf16[256,1408]{1,0:T(8,128)(2,1)S(1)}, u32[]{:S(2)}, u32[]{:S(2)}) collective-permute-start(bf16[256,1408]{1,0:T(8,128)(2,1)S(1)} %compact.1.own_ref), channel_id=1, source_target_pairs={{0,1},{1,0},{2,3},{3,2},{4,5},{5,4},{6,7},{7,6},{8,9},{9,8},{10,11... | collective-permute-start | bytes 2162696 | tf_op jit(solution)/shard_map/ppermute | solution.py:386
  45.5 35.3 %copy-start = (bf16[400,512]{1,0:T(8,128)(2,1)S(1)}, bf16[400,512]{1,0:T(8,128)(2,1)}, u32[]{:S(2)}) copy-start(bf16[400,512]{1,0:T(8,128)(2,1)} %constant.34.clone.table_ref) | copy-start | bytes 1228804
  45.5 35.3 %all-to-all-start.1 = ((bf16[128,48,128]{2,1,0:T(8,128)(2,1)}), bf16[128,48,128]{2,1,0:T(8,128)(2,1)S(1)}, u32[]{:S(2)}, u32[]{:S(2)}) async-start(bf16[128,48,128]{2,1,0:T(8,128)(2,1)} %get-tuple-element.14), calls=%async_computation.1 | async-start | bytes 3145728 | tf_op jit(solution)/shard_map/all_to_all | solution.py:378
  53.3 21.2 %collective-permute-start.1 = (bf16[4,16,128]{2,1,0:T(8,128)(2,1)S(1)}, bf16[4,16,128]{2,1,0:T(8,128)(2,1)S(1)}, u32[]{:S(2)}, u32[]{:S(2)}) collective-permute-start(bf16[4,16,128]{2,1,0:T(8,128)(2,1)S(1)} %get-tuple-element.16), channel_id=1, source_target_pairs={{0,4},{4,8},{8,12},{12,0},{16,20},{20,24},{24,28},{28,16},{32,36},... | collective-permute-start | bytes 49160 | tf_op jit(solution)/shard_map/ppermute | solution.py:390
  54.8 19.7 %collective-permute-start.2 = (bf16[4,16,128]{2,1,0:T(8,128)(2,1)S(1)}, bf16[4,16,128]{2,1,0:T(8,128)(2,1)S(1)}, u32[]{:S(2)}, u32[]{:S(2)}) collective-permute-start(bf16[4,16,128]{2,1,0:T(8,128)(2,1)S(1)} %get-tuple-element.17), channel_id=1, source_target_pairs={{0,8},{4,12},{8,0},{12,4},{16,24},{20,28},{24,16},{28,20},{32,40},... | collective-permute-start | bytes 49160 | tf_op jit(solution)/shard_map/ppermute | solution.py:390
  57.7 16.8 %collective-permute-start.3 = (bf16[4,16,128]{2,1,0:T(8,128)(2,1)S(1)}, bf16[4,16,128]{2,1,0:T(8,128)(2,1)S(1)}, u32[]{:S(2)}, u32[]{:S(2)}) collective-permute-start(bf16[4,16,128]{2,1,0:T(8,128)(2,1)S(1)} %get-tuple-element.18), channel_id=1, source_target_pairs={{0,12},{4,0},{8,4},{12,8},{16,28},{20,16},{24,20},{28,24},{32,44},... | collective-permute-start | bytes 49160 | tf_op jit(solution)/shard_map/ppermute | solution.py:390

commit v8 on v7

--- a/solution.py
+++ b/solution.py
@@ -342,7 +342,7 @@
 
 
 def lag_transform(info, stacks, rest, devices):
-    parts = 8
+    parts = 16
     table = jnp.asarray(lag_rows(devices))
     shape = (2, 16, 64, LAGS)
     out = pl.pallas_call(

time: 84.7 us -> 84.4 us (level)
  no operation moved by 1% of the time
where the time goes in v8:
time: 84.4 us; the launch traced here: 84.2 us
  blocking collectives  40.2 us (48%)
  waiting for transfers between devices  15.9 us (19%)
  starting transfers between devices  14.1 us (17%)
  Pallas kernels  13.8 us (16%)
    all_to_all x1, blocking collectives, exchange(): return lax.all_to_all(array, axes, split_axis=0, concat_axis=0, tiled=True)  34 us
    ppermute x3, waiting for transfers between devices, per_device(): lax.ppermute(rest[n], 'chan', [(c, c // 4 * 4 + (c + n) % 4) for c in ran...  15.9 us
    all_to_all x1, starting transfers between devices, exchange(): return lax.all_to_all(array, axes, split_axis=0, concat_axis=0, tiled=True)  7.77 us
    all_gather x1, blocking collectives, per_device(): rest = lax.all_gather(jnp.concatenate(rest), 'win')  6.27 us
    ppermute x3, starting transfers between devices, per_device(): lax.ppermute(rest[n], 'chan', [(c, c // 4 * 4 + (c + n) % 4) for c in ran...  5.37 us
    pallas_call x1, Pallas kernels, whiten(): pl.pallas_call(functools.partial(whiten_kernel, devices), in_specs=[pl.Bl...  5.13 us
    pallas_call x1, Pallas kernels, lag_transform(): pl.pallas_call(functools.partial(lag_kernel, parts), grid=(1,), in_specs=...  3.39 us
    pallas_call x1, Pallas kernels, stack_shared(): pl.pallas_call(shared_kernel, out_shape=[jax.ShapeDtypeStruct(shape, jnp....  2.64 us
  transfers between devices with their start and end apart: 5, of which 1 were waited for; matrix products, arithmetic and copies ran while one was open for 0% of the time, Pallas kernels for 3%

profile of v8, /device:TPU:21, one launch (start us, length us, event | category | flops | bytes accessed | tf_op | source)
XLA Modules:
  0.0 84.2 jit_solution(16561148321701072306)
XLA Ops:
  0.0 5.1 %whiten.1 = bf16[1024,896]{1,0:T(8,128)(2,1)S(1)} custom-call(bf16[2,1000,1024]{2,1,0:T(8,128)(2,1)} %records_hbm.1), custom_call_target="tpu_custom_call" | custom-call | flops 1638400000 | bytes 6193152 | tf_op jit(solution)/shard_map/whiten/pallas_call | solution.py:122
  5.2 0.1 pad_add_fusion.info_ref
  5.2 34.0 %all_to_all.10 = bf16[128,8,896]{2,1,0:T(8,128)(2,1)S(1)} all-to-all(bf16[128,8,896]{2,1,0:T(8,128)(2,1)S(1)} %bitcast.11), channel_id=1, replica_groups=mesh['chan'=32,'win'=4] {'chan','win'}, dimensions={0} | all-to-all | bytes 3670016 | tf_op jit(solution)/shard_map/all_to_all | solution.py:378
  39.2 0.5 compact.1.own_ref
  39.7 1.0 %collective-permute-start = (bf16[256,1408]{1,0:T(8,128)(2,1)S(1)}, bf16[256,1408]{1,0:T(8,128)(2,1)S(1)}, u32[]{:S(2)}, u32[]{:S(2)}) collective-permute-start(bf16[256,1408]{1,0:T(8,128)(2,1)S(1)} %compact.1.own_ref), channel_id=1, source_target_pairs={{0,1},{1,0},{2,3},{3,2},{4,5},{5,4},{6,7},{7,6},{8,9},{9,8},{10,11... | collective-permute-start | bytes 2162696 | tf_op jit(solution)/shard_map/ppermute | solution.py:386
  40.7 2.1 %stack.17.items_ref = bf16[128,32,128]{2,1,0:T(8,128)(2,1)S(1)} custom-call(bf16[1024,896]{1,0:T(8,128)(2,1)S(1)} %bitcast.9), custom_call_target="tpu_custom_call" | custom-call | flops 1073741824 | bytes 4194304 | tf_op jit(solution)/shard_map/stack/pallas_call | solution.py:244
  42.8 0.0 collective-permute-done.other_ref
  42.8 2.6 %stack_shared.1 = (bf16[128,48,128]{2,1,0:T(8,128)(2,1)}, bf16[4,16,128]{2,1,0:T(8,128)(2,1)S(1)}, bf16[4,16,128]{2,1,0:T(8,128)(2,1)S(1)}, bf16[4,16,128]{2,1,0:T(8,128)(2,1)S(1)}, bf16[4,16,128]{2,1,0:T(8,128)(2,1)S(1)}) custom-call(s32[3]{0:T(128)S(1)} %pad_add_fusion.info_ref, bf16[256,1408]{1,0:T(8,128)(2,1)S(1)} %compact.1.own_ref, ...), custom_call_target="tpu_custom_call" | custom-call | flops 536870912 | bytes 4194304 | tf_op jit(solution)/shard_map/stack_shared/pallas_call | solution.py:297
  45.5 0.0 copy-start
  45.5 7.8 %all-to-all-start.1 = ((bf16[128,48,128]{2,1,0:T(8,128)(2,1)}), bf16[128,48,128]{2,1,0:T(8,128)(2,1)S(1)}, u32[]{:S(2)}, u32[]{:S(2)}) async-start(bf16[128,48,128]{2,1,0:T(8,128)(2,1)} %get-tuple-element.14), calls=%async_computation.1 | async-start | bytes 3145728 | tf_op jit(solution)/shard_map/all_to_all | solution.py:378
  53.3 1.5 %collective-permute-start.1 = (bf16[4,16,128]{2,1,0:T(8,128)(2,1)S(1)}, bf16[4,16,128]{2,1,0:T(8,128)(2,1)S(1)}, u32[]{:S(2)}, u32[]{:S(2)}) collective-permute-start(bf16[4,16,128]{2,1,0:T(8,128)(2,1)S(1)} %get-tuple-element.16), channel_id=1, source_target_pairs={{0,4},{4,8},{8,12},{12,0},{16,20},{20,24},{24,28},{28,16},{32,36},... | collective-permute-start | bytes 49160 | tf_op jit(solution)/shard_map/ppermute | solution.py:390
  54.8 2.9 %collective-permute-start.2 = (bf16[4,16,128]{2,1,0:T(8,128)(2,1)S(1)}, bf16[4,16,128]{2,1,0:T(8,128)(2,1)S(1)}, u32[]{:S(2)}, u32[]{:S(2)}) collective-permute-start(bf16[4,16,128]{2,1,0:T(8,128)(2,1)S(1)} %get-tuple-element.17), channel_id=1, source_target_pairs={{0,8},{4,12},{8,0},{12,4},{16,24},{20,28},{24,16},{28,20},{32,40},... | collective-permute-start | bytes 49160 | tf_op jit(solution)/shard_map/ppermute | solution.py:390
  57.7 0.9 %collective-permute-start.3 = (bf16[4,16,128]{2,1,0:T(8,128)(2,1)S(1)}, bf16[4,16,128]{2,1,0:T(8,128)(2,1)S(1)}, u32[]{:S(2)}, u32[]{:S(2)}) collective-permute-start(bf16[4,16,128]{2,1,0:T(8,128)(2,1)S(1)} %get-tuple-element.18), channel_id=1, source_target_pairs={{0,12},{4,0},{8,4},{12,8},{16,28},{20,16},{24,20},{28,24},{32,44},... | collective-permute-start | bytes 49160 | tf_op jit(solution)/shard_map/ppermute | solution.py:390
  58.6 15.8 %collective-permute-done.1 = bf16[4,16,128]{2,1,0:T(8,128)(2,1)S(1)} collective-permute-done((bf16[4,16,128]{2,1,0:T(8,128)(2,1)S(1)}, bf16[4,16,128]{2,1,0:T(8,128)(2,1)S(1)}, u32[]{:S(2)}, u32[]{:S(2)}) %collective-permute-start.1) | collective-permute-done | bytes 16416 | tf_op jit(solution)/shard_map/ppermute | solution.py:390
  74.5 0.0 collective-permute-done.2
  74.5 0.0 collective-permute-done.3
  74.5 6.3 %all-gather = bf16[64,16,128]{2,1,0:T(8,128)(2,1)S(1)} all-gather(bf16[16,16,128]{2,1,0:T(8,128)(2,1)S(1)} %pad_maximum_fusion), channel_id=2, replica_groups=mesh['chan'=32,'win'=4] {'win'}, dimensions={0}, use_global_device_ids=true | all-gather | bytes 327680 | tf_op jit(solution)/shard_map/all_gather | solution.py:391
  80.8 0.0 all-to-all-done.1
  80.8 0.0 copy-done
  80.8 3.4 %lag_transform.1 = f32[2,16,64,256]{3,2,1,0:T(8,128)} custom-call(s32[3]{0:T(128)S(1)} %pad_add_fusion.info_ref, bf16[400,512]{1,0:T(8,128)(2,1)S(1)} %copy-done, bf16[6144,128]{1,0:T(8,128)(2,1)S(1)} %bitcast.10, bf16[4,16,16,128]{3,2,1,0:T(8,128)(2,1)S(1)} %bitcast.12), custom_call_target="tpu_custom_call" | custom-call | flops 838860800 | bytes 4194304 | tf_op jit(solution)/shard_map/lag_transform/pallas_call | solution.py:348
  (1 shorter events, 0.0 us)
Async XLA Ops:
  39.7 3.1 %collective-permute-start = (bf16[256,1408]{1,0:T(8,128)(2,1)S(1)}, bf16[256,1408]{1,0:T(8,128)(2,1)S(1)}, u32[]{:S(2)}, u32[]{:S(2)}) collective-permute-start(bf16[256,1408]{1,0:T(8,128)(2,1)S(1)} %compact.1.own_ref), channel_id=1, source_target_pairs={{0,1},{1,0},{2,3},{3,2},{4,5},{5,4},{6,7},{7,6},{8,9},{9,8},{10,11... | collective-permute-start | bytes 2162696 | tf_op jit(solution)/shard_map/ppermute | solution.py:386
  45.5 35.3 %copy-start = (bf16[400,512]{1,0:T(8,128)(2,1)S(1)}, bf16[400,512]{1,0:T(8,128)(2,1)}, u32[]{:S(2)}) copy-start(bf16[400,512]{1,0:T(8,128)(2,1)} %constant.34.clone.table_ref) | copy-start | bytes 1228804
  45.5 35.3 %all-to-all-start.1 = ((bf16[128,48,128]{2,1,0:T(8,128)(2,1)}), bf16[128,48,128]{2,1,0:T(8,128)(2,1)S(1)}, u32[]{:S(2)}, u32[]{:S(2)}) async-start(bf16[128,48,128]{2,1,0:T(8,128)(2,1)} %get-tuple-element.14), calls=%async_computation.1 | async-start | bytes 3145728 | tf_op jit(solution)/shard_map/all_to_all | solution.py:378
  53.3 21.2 %collective-permute-start.1 = (bf16[4,16,128]{2,1,0:T(8,128)(2,1)S(1)}, bf16[4,16,128]{2,1,0:T(8,128)(2,1)S(1)}, u32[]{:S(2)}, u32[]{:S(2)}) collective-permute-start(bf16[4,16,128]{2,1,0:T(8,128)(2,1)S(1)} %get-tuple-element.16), channel_id=1, source_target_pairs={{0,4},{4,8},{8,12},{12,0},{16,20},{20,24},{24,28},{28,16},{32,36},... | collective-permute-start | bytes 49160 | tf_op jit(solution)/shard_map/ppermute | solution.py:390
  54.8 19.7 %collective-permute-start.2 = (bf16[4,16,128]{2,1,0:T(8,128)(2,1)S(1)}, bf16[4,16,128]{2,1,0:T(8,128)(2,1)S(1)}, u32[]{:S(2)}, u32[]{:S(2)}) collective-permute-start(bf16[4,16,128]{2,1,0:T(8,128)(2,1)S(1)} %get-tuple-element.17), channel_id=1, source_target_pairs={{0,8},{4,12},{8,0},{12,4},{16,24},{20,28},{24,16},{28,20},{32,40},... | collective-permute-start | bytes 49160 | tf_op jit(solution)/shard_map/ppermute | solution.py:390
  57.7 16.8 %collective-permute-start.3 = (bf16[4,16,128]{2,1,0:T(8,128)(2,1)S(1)}, bf16[4,16,128]{2,1,0:T(8,128)(2,1)S(1)}, u32[]{:S(2)}, u32[]{:S(2)}) collective-permute-start(bf16[4,16,128]{2,1,0:T(8,128)(2,1)S(1)} %get-tuple-element.18), channel_id=1, source_target_pairs={{0,12},{4,0},{8,4},{12,8},{16,28},{20,16},{24,20},{28,24},{32,44},... | collective-permute-start | bytes 49160 | tf_op jit(solution)/shard_map/ppermute | solution.py:390
